TPU v7x, 128 devices: a whole 4x4x4 slice. The times are simulated.
128 devices in a mesh: row: 4 (over z), col: 32 (over x, y, core).
Axes of the slice: x: 4, y: 4, z: 4, core: 2. Of those that a mesh axis runs over, the one named last changes fastest.
Arguments:
- splat_params: float32 [10, 8388608], P(None, ('row', 'col')), as said below
- list_owner: int32 [512, 1024, 1], P(('row', 'col')), may hold values from 0 to 127; in each aligned block of 4096 rows (0 to 4095, 4096 to 8191, ..., all dimensions but the last counted through in order) at most 64 rows name the same one
- list_slot: int32 [512, 1024], P(('row', 'col')), may hold values from 0 to 65535
- list_length: int32 [512], P(('row', 'col')), may hold values from 512 to 1024, as said below
- target: float32 [4, 512, 256], P(None, ('row', 'col')), may hold values from 0 to 1
Outputs:
- rendered: float32 [4, 512, 256], P(None, ('row', 'col'))
- splat_grads: float32 [10, 8388608], P(None, ('row', 'col'))
Inputs may be any that keep to these rules, and one draw needn't show every extreme that they name: `list_owner`: within the entries of one device's tiles (aligned blocks of 4096 entries), no owner is named more than 64 times, a bound that some block reaches. `list_length`: some tile has exactly 1024 live entries; every tile has at least 512. `splat_params`: conic entries satisfy a > 0, c > 0 and b * b < a * c; opacity lies in (0, 0.02]; colours and depth lie in [0, 1].
All inputs are finite; a program needn't handle non-finite values.
Results may differ from a plain program's by a relative error of at most 0.0003.
Values sent between devices are 32-bit elements; how exact they have to be, the bound alone decides.
No kernel may reach another device: no remote copies, remote signals or barrier semaphores. Data moves between devices by JAX's collectives and lax.ppermute only.
A program may use at most 128 MiB of HBM per device.

v0:
```python
import jax
import jax.numpy as jnp
from jax import lax
from jax.experimental import pallas as pl
from jax.experimental.pallas import tpu as pltpu
from jax.sharding import PartitionSpec as P

AXES = ("row", "col")
DEVS = 128
RANKS = 64
TILES = 4
SEGS = 128
STEPS = 8
ROWS = TILES * STEPS
WIRE = 5
GROUP = 16
BLOCK = 16
CHUNKS = ((0, 32), (32, 48), (48, 64))
CLOSE = 1024
CHAINS = 4
LOG2E = 1.4426950408889634
F32 = jnp.float32
BF16 = jnp.bfloat16


def iota(shape, dim):
    return lax.broadcasted_iota(jnp.int32, shape, dim)


def dot(a, b):
    return lax.dot_general(a, b, (((1,), (0,)), ((), ())), preferred_element_type=F32)


def dot_nt(a, b):
    return lax.dot_general(a, b, (((1,), (1,)), ((), ())), preferred_element_type=F32)


def split(x, parts):
    out = []
    for _ in range(parts - 1):
        head = x.astype(BF16)
        out.append(head)
        x = x - head.astype(F32)
    out.append(x.astype(BF16))
    return out


def onehot_rows(row, count):
    wide = jnp.broadcast_to(row, (count, row.shape[1]))
    return wide == iota(wide.shape, 0).astype(F32)


def route_kernel(length_ref, owner_ref, slot_ref, request_ref, owner_out, rank_out):
    lane = iota((STEPS, SEGS), 1)
    step = iota((STEPS, SEGS), 0)
    picks = (lane & (STEPS - 1)) == step
    pieces = []
    for r in range(STEPS):
        rows = []
        slot_rows = []
        for t in range(TILES):
            own = jnp.broadcast_to(owner_ref[t * STEPS + r : t * STEPS + r + 1, :], (STEPS, SEGS))
            rows.append(jnp.where(picks, own, 0))
            slot = slot_ref[t : t + 1, r * SEGS : (r + 1) * SEGS]
            slot_rows.append(jnp.where(picks, jnp.broadcast_to(slot, (STEPS, SEGS)), 0))
        rows += [s >> 8 for s in slot_rows] + [s & 255 for s in slot_rows]
        pieces.append(jnp.concatenate(rows, axis=0).astype(F32).astype(BF16))
    spread = jnp.concatenate(pieces, axis=1)
    place = ((iota((STEPS * SEGS, SEGS), 0) >> 3) == iota((STEPS * SEGS, SEGS), 1)).astype(F32)
    moved = dot(spread, place.astype(BF16))
    lane = iota((ROWS, SEGS), 1)
    row = iota((ROWS, SEGS), 0)
    length = jnp.full((ROWS, SEGS), length_ref[0], jnp.int32)
    for t in range(1, TILES):
        length = jnp.where((row >> 3) == t, length_ref[t], length)
    live = (lane * STEPS + (row & (STEPS - 1))) < length
    owners = jnp.where(live, moved[0:ROWS], -1.0)
    high = moved[ROWS : 2 * ROWS]
    low = moved[2 * ROWS : 3 * ROWS]
    owner_out[...] = owners
    before = (iota((256, 256), 0) < iota((256, 256), 1)).astype(F32).astype(BF16)
    before = jnp.concatenate([before, jnp.ones((256, 256), BF16)], axis=1)
    rank_of = (iota((2 * RANKS, 256), 0) & (RANKS - 1)).astype(F32)
    upper = iota((2 * RANKS, 256), 0) < RANKS
    carry = jnp.zeros((DEVS, 256), F32)
    request = jnp.zeros((2 * RANKS, DEVS), F32)
    for n in range(ROWS // 2):
        pair = lambda x: jnp.concatenate([x[2 * n : 2 * n + 1], x[2 * n + 1 : 2 * n + 2]], axis=1)
        hot = onehot_rows(pair(owners), DEVS)
        hot16 = hot.astype(F32).astype(BF16)
        counted = dot(hot16, before)
        rank = jnp.sum(jnp.where(hot, counted[:, :256] + carry, 0.0), axis=0, keepdims=True)
        carry = carry + counted[:, 256:]
        rank_out[2 * n : 2 * n + 1, :] = rank[:, :SEGS]
        rank_out[2 * n + 1 : 2 * n + 2, :] = rank[:, SEGS:]
        values = jnp.where(upper, pair(high), pair(low))
        values = jnp.where(rank_of == rank, values, 0.0)
        request = request + dot_nt(values.astype(BF16), hot16)
    slots = request[:RANKS] * 256.0 + request[RANKS:]
    slots = jnp.concatenate([slots, slots], axis=0).T
    full = jnp.where(iota((DEVS, DEVS), 1) < RANKS, slots, carry[:, :DEVS])
    request_ref[...] = full.astype(jnp.int32)


def pack_kernel(*refs):
    out_ref = refs[-1]
    pad = jnp.zeros((GROUP - 10, 128), F32)
    for n in range(refs[0].shape[1] // 128):
        blocks = []
        for ref in refs[:-1]:
            blocks += [ref[:, n * 128 : (n + 1) * 128], pad]
        out_ref[n * 128 : (n + 1) * 128, :] = jnp.concatenate(blocks, axis=0).T


def bit_clear(shift):
    return (iota((RANKS, 128), 1) & shift) == 0


def merge_groups(xs):
    xs = [xs[q] for q in (0, 4, 2, 6, 1, 5, 3, 7)]
    for shift in (16, 32, 64):
        half = len(xs) // 2
        low = bit_clear(shift)
        xs = [
            jnp.where(low, x, y) + pltpu.roll(jnp.where(low, y, x), shift, 1)
            for x, y in zip(xs[:half], xs[half:])
        ]
    return xs[0]


def spread_groups(x):
    xs = [x]
    for shift in (64, 32, 16):
        low = bit_clear(shift)
        nexts = []
        for y in xs:
            z = pltpu.roll(y, shift, 1)
            nexts += [jnp.where(low, y, z), jnp.where(low, z, y)]
        xs = nexts
    return xs


def prepare(asked_ref, table_rows, row_number_ref, number_ref, number_sem, group_ref, widen_ref):
    asked = asked_ref[...]
    lane = iota((DEVS, 128), 1)
    row_number_ref[...] = jnp.where(lane < RANKS, asked & (table_rows - 1), asked)
    copy = pltpu.make_async_copy(row_number_ref, number_ref, number_sem)
    copy.start()
    groups = lax.div(asked, table_rows).astype(F32).T[:RANKS]
    for b in range(DEVS // BLOCK):
        turned = groups if b == 0 else pltpu.roll(groups, DEVS - b * BLOCK, 1)
        group_ref[b * RANKS : (b + 1) * RANKS, :] = turned.astype(BF16)
    for n in range(BLOCK):
        widen_ref[:, n * 128 : (n + 1) * 128] = (iota((DEVS, 128), 0) == n).astype(F32).astype(BF16)
    return copy


def wide_groups(group_ref, widen_ref, b):
    at = pl.ds(pl.multiple_of(b * RANKS, RANKS), RANKS)
    return dot(group_ref[at, :], widen_ref[...])


def gather_kernel(
    asked_ref, table_hbm, out_ref, row_number_ref, number_ref, group_ref, widen_ref, row_ref, table_ref, sems
):
    left = iota((WIRE, 128), 1) < RANKS
    fill = pltpu.make_async_copy(table_hbm, table_ref, sems.at[1])
    fill.start()
    copy = prepare(asked_ref, table_ref.shape[0], row_number_ref, number_ref, sems.at[0], group_ref, widen_ref)
    row_ref[...] = jnp.zeros(row_ref.shape, F32)
    copy.wait()
    fill.wait()

    def block(b, carry):
        def source(q, carry):
            src = b * BLOCK + q
            count = number_ref[src, RANKS]
            mine_ref = row_ref.at[pl.ds(pl.multiple_of(q * RANKS, RANKS), RANKS)]
            for first, last in CHUNKS:

                @pl.when(count > first)
                def _():
                    for rank in range(first, last):
                        mine_ref[rank : rank + 1, :] = table_ref[pl.ds(number_ref[src, rank], 1), :]

            return carry

        lax.fori_loop(0, BLOCK, source, 0)
        groups = wide_groups(group_ref, widen_ref, b)
        lane_group = (iota((RANKS, 128), 1) >> 4).astype(F32)
        halves = []
        for half in range(2):
            picked = []
            for n in range(half * 8, half * 8 + 8):
                rows = row_ref[n * RANKS : (n + 1) * RANKS, :]
                picked.append(jnp.where(lane_group == groups[:, n * 128 : (n + 1) * 128], rows, 0.0))
            halves.append(merge_groups(picked))
        turned = jnp.concatenate(halves, axis=0).T
        evens, odds = [], []
        for q in range(8):
            first = turned[q * GROUP : q * GROUP + WIRE]
            second = turned[q * GROUP + WIRE : q * GROUP + 2 * WIRE]
            evens.append(jnp.where(left, first, pltpu.roll(second, RANKS, 1)))
            odds.append(jnp.where(left, pltpu.roll(first, RANKS, 1), second))
        at = pl.multiple_of(b * BLOCK * WIRE, 8)
        out_ref[pl.ds(at, BLOCK * WIRE), :] = jnp.concatenate(evens + odds, axis=0)
        return carry

    lax.fori_loop(0, DEVS // BLOCK, block, 0)


def scatter_kernel(
    asked_ref, wire_ref, out_hbm, row_number_ref, number_ref, group_ref, widen_ref, row_ref,
    turn_ref, out_ref, sems, *totals,
):
    left = iota((WIRE, 128), 1) < RANKS
    table_rows = totals[0].shape[0]
    copy = prepare(asked_ref, table_rows, row_number_ref, number_ref, sems.at[0], group_ref, widen_ref)
    turn_ref[...] = jnp.zeros((128, 128), F32)

    def clear(i, carry):
        for ref in totals:
            ref[pl.ds(pl.multiple_of(i * 256, 256), 256), :] = jnp.zeros((256, 128), F32)
        return carry

    lax.fori_loop(0, table_rows // 256, clear, 0)
    copy.wait()

    def block(b, carry):
        at = pl.multiple_of(b * BLOCK * WIRE, 8)
        wire = wire_ref[pl.ds(at, BLOCK * WIRE), :]
        for q in range(8):
            even = wire[q * WIRE : (q + 1) * WIRE]
            odd = wire[(q + 8) * WIRE : (q + 9) * WIRE]
            turn_ref[q * GROUP : q * GROUP + WIRE, :] = jnp.where(left, even, pltpu.roll(odd, RANKS, 1))
            turn_ref[q * GROUP + WIRE : q * GROUP + 2 * WIRE, :] = jnp.where(left, pltpu.roll(even, RANKS, 1), odd)
        turned = turn_ref[...].T
        groups = wide_groups(group_ref, widen_ref, b)
        lane_group = (iota((RANKS, 128), 1) >> 4).astype(F32)
        for half in range(2):
            spreads = spread_groups(turned[half * RANKS : (half + 1) * RANKS])
            for q in range(8):
                n = half * 8 + q
                row_ref[n * RANKS : (n + 1) * RANKS, :] = jnp.where(
                    lane_group == groups[:, n * 128 : (n + 1) * 128], spreads[q], 0.0
                )

        def source(q, carry):
            src = b * BLOCK + q
            count = number_ref[src, RANKS]
            mine_ref = row_ref.at[pl.ds(pl.multiple_of(q * RANKS, RANKS), RANKS)]
            for first, last in CHUNKS:

                @pl.when(count > first)
                def _():
                    for start in range(first, last, CHAINS):
                        news = []
                        for i, ref in enumerate(totals):
                            row = number_ref[src, start + i]
                            news.append((row, mine_ref[start + i : start + i + 1, :] + ref[pl.ds(row, 1), :]))
                        for ref, (row, total) in zip(totals, news):
                            ref[pl.ds(row, 1), :] = total

            return carry

        lax.fori_loop(0, BLOCK, source, 0)
        return carry

    lax.fori_loop(0, DEVS // BLOCK, block, 0)

    def close(i, carry):
        base = pl.multiple_of(i * CLOSE, CLOSE)
        for n in range(CLOSE // 128):
            at = pl.ds(base + n * 128, 128)
            total = totals[0][at, :]
            for ref in totals[1:]:
                total = total + ref[at, :]
            total = total.T
            for g in range(8):
                out_ref[:, pl.ds(g * table_rows + base + n * 128, 128)] = total[g * GROUP : g * GROUP + 10]
        for g in range(8):
            lanes = pl.ds(pl.multiple_of(g * table_rows + base, CLOSE), CLOSE)
            pltpu.make_async_copy(out_ref.at[:, lanes], out_hbm.at[:, lanes], sems.at[1]).start()
        return carry

    lax.fori_loop(0, table_rows // CLOSE, close, 0)
    pltpu.make_async_copy(out_ref, out_hbm, sems.at[1]).wait()


def render_kernel(
    wire_ref, owner_ref, rank_ref, target_ref, image_ref, out_ref,
    hot_ref, left_ref, value_ref, fall_ref, flow_ref, sum_ref, keep_ref, reach_ref, behind_ref,
    shade_ref, column_ref, picture_ref, across_ref, tilt_ref, grad_ref, spread_ref,
):
    for c in range(WIRE):
        block = wire_ref[pl.ds(c, DEVS, stride=WIRE), :].T
        parts = split(block, 3)
        left_ref[c * 128 : (c + 1) * 128, :] = jnp.concatenate(parts, axis=1)
    rank_of = iota((RANKS, 256), 0).astype(F32)

    def fetch(n, carry):
        at = pl.ds(pl.multiple_of(n * 256, 256), 256)
        owner = jnp.concatenate([owner_ref[pl.ds(2 * n, 1), :], owner_ref[pl.ds(2 * n + 1, 1), :]], axis=1)
        rank = jnp.concatenate([rank_ref[pl.ds(2 * n, 1), :], rank_ref[pl.ds(2 * n + 1, 1), :]], axis=1)
        hot = onehot_rows(owner, DEVS).astype(F32).astype(BF16)
        hot_ref[:, at] = hot
        mine = rank_of == rank
        found = dot(left_ref[...], jnp.concatenate([hot, hot, hot], axis=0))
        for c in range(WIRE):
            for h in range(2):
                block = found[c * 128 + h * RANKS : c * 128 + (h + 1) * RANKS]
                got = jnp.sum(jnp.where(mine, block, 0.0), axis=0, keepdims=True)
                v = c + WIRE * h
                value_ref[v, pl.ds(2 * n, 1), :] = got[:, :SEGS]
                value_ref[v, pl.ds(2 * n + 1, 1), :] = got[:, SEGS:]
        return carry

    lax.fori_loop(0, ROWS // 2, fetch, 0)

    flat = jnp.concatenate([target_ref[ch] for ch in range(4)] + [jnp.zeros((112, 256), F32)], axis=0)
    column_ref[...] = jnp.concatenate([flat[:, :128].T, flat[:, 128:].T], axis=0)
    picture_ref[...] = jnp.zeros((256, 128), F32)
    earlier = (iota((128, 128), 0) < iota((128, 128), 1)).astype(F32).astype(BF16)
    later = (iota((128, 128), 0) > iota((128, 128), 1)).astype(F32).astype(BF16)
    ones = jnp.ones((256, 128), BF16)
    earlier = jnp.concatenate([earlier, earlier, earlier], axis=0)
    later = jnp.concatenate([later, later], axis=0)
    pixel_x = iota((16, SEGS), 0).astype(F32) + 0.5

    def tile(t, carry):
        first = t * STEPS
        for k in range(STEPS):
            value = lambda v: value_ref[v, pl.ds(first + k, 1), :]
            offset_x = pixel_x - value(0)
            across_ref[k] = (-0.5 * LOG2E) * value(2) * offset_x * offset_x
            tilt_ref[k] = -LOG2E * value(3) * offset_x

        def forward(n, carry):
            for half in range(2):
                y = 2 * n + half
                pixel_y = y.astype(F32) + 0.5
                keep = jnp.ones((16, SEGS), F32)
                sums = [jnp.zeros((16, SEGS), F32) for _ in range(4)]
                at = pl.ds(pl.multiple_of(y * 16, 16), 16)
                for k in range(STEPS):
                    value = lambda v: value_ref[v, pl.ds(first + k, 1), :]
                    offset_y = pixel_y - value(1)
                    down = (-0.5 * LOG2E) * value(4) * offset_y * offset_y
                    fall = jnp.exp2(across_ref[k] + down + tilt_ref[k] * offset_y)
                    flow = fall * keep
                    weight = value(5) * flow
                    keep = keep - weight
                    for ch in range(4):
                        sums[ch] = sums[ch] + value(6 + ch) * weight
                    fall_ref[k, at, :] = fall
                    flow_ref[k, at, :] = flow
                keep_ref[at, :] = keep
                for ch in range(4):
                    sum_ref[ch, at, :] = sums[ch]
            return carry

        lax.fori_loop(0, 8, forward, 0)

        keep = keep_ref[...]
        logs = jnp.concatenate(split(jnp.log(keep), 3), axis=1)
        reach = jnp.exp(dot(logs, earlier))
        reach_ref[...] = reach
        spent = jnp.zeros((256, SEGS), F32)
        for ch in range(4):
            part = sum_ref[ch] * reach
            rendered = dot(jnp.concatenate(split(part, 2), axis=1), ones)
            here = iota((256, 128), 1) == ch * TILES + t
            wanted = jnp.sum(jnp.where(here, column_ref[...], 0.0), axis=1, keepdims=True)
            shade = 2.0 * (rendered - wanted)
            picture_ref[...] = jnp.where(here, rendered, picture_ref[...])
            shade_ref[ch] = shade
            spent = spent + shade * part
        rest = dot(jnp.concatenate(split(spent, 2), axis=1), later)
        behind_ref[...] = rest / (reach * keep)

        for k in reversed(range(STEPS)):
            value = lambda v: value_ref[v, pl.ds(first + k, 1), :]
            mean_y = jnp.broadcast_to(value(1), (8, SEGS))
            opacity = jnp.broadcast_to(value(5), (8, SEGS))
            colours = [jnp.broadcast_to(value(6 + ch), (8, SEGS)) for ch in range(4)]

            def backward(n, sums):
                zero, one, two, tints = sums
                zero, one, two, tints = list(zero), list(one), list(two), list(tints)
                for quarter in range(2):
                    y = 2 * n + quarter
                    offset_y = y.astype(F32) + 0.5 - mean_y
                    for half in range(2):
                        at = pl.ds(pl.multiple_of(y * 16 + half * 8, 8), 8)
                        shades = [shade_ref[ch, at, :] for ch in range(4)]
                        flow = flow_ref[k, at, :] * reach_ref[at, :]
                        lit = (shades[0] * colours[0] + shades[1] * colours[1]) + (
                            shades[2] * colours[2] + shades[3] * colours[3]
                        )
                        behind = behind_ref[at, :]
                        gap = lit - behind
                        behind_ref[at, :] = behind + opacity * fall_ref[k, at, :] * gap
                        grad = flow * gap
                        slope = grad * offset_y
                        zero[half] = zero[half] + grad
                        one[half] = one[half] + slope
                        two[half] = two[half] + slope * offset_y
                        for ch in range(4):
                            tints[ch] = tints[ch] + flow * shades[ch]
                return (tuple(zero), tuple(one), tuple(two), tuple(tints))

            blank = jnp.zeros((8, SEGS), F32)
            zero, one, two, tints = lax.fori_loop(
                0, 8, backward, ((blank,) * 2, (blank,) * 2, (blank,) * 2, (blank,) * 4)
            )
            total = lambda x: jnp.sum(x, axis=0, keepdims=True)
            offset_x = pixel_x - value(0)
            near, far = offset_x[:8], offset_x[8:]
            sum_0 = total(zero[0] + zero[1])
            slope_x = (near * zero[0], far * zero[1])
            sum_x = total(slope_x[0] + slope_x[1])
            sum_xx = total(near * slope_x[0] + far * slope_x[1])
            sum_y = total(one[0] + one[1])
            sum_xy = total(near * one[0] + far * one[1])
            sum_yy = total(two[0] + two[1])
            opacity = value(5)
            grads = [
                opacity * (value(2) * sum_x + value(3) * sum_y),
                opacity * (value(4) * sum_y + value(3) * sum_x),
                -0.5 * opacity * sum_xx,
                -opacity * sum_xy,
                -0.5 * opacity * sum_yy,
                sum_0,
            ] + [opacity * total(tint) for tint in tints]
            for v in range(10):
                grad_ref[v, pl.ds(first + k, 1), :] = grads[v]
        return carry

    lax.fori_loop(0, TILES, tile, 0)

    picture = picture_ref[...]
    picture = jnp.concatenate([picture[:128].T, picture[128:].T], axis=1)
    for ch in range(4):
        image_ref[ch] = picture[ch * TILES : (ch + 1) * TILES, :]

    spread_ref[...] = jnp.zeros((WIRE * 128, DEVS), F32)

    def spread(n, carry):
        at = pl.ds(pl.multiple_of(n * 256, 256), 256)
        rank = jnp.concatenate([rank_ref[pl.ds(2 * n, 1), :], rank_ref[pl.ds(2 * n + 1, 1), :]], axis=1)
        mine = rank_of == rank
        hot = hot_ref[:, at]
        rows = []
        for c in range(WIRE):
            for h in range(2):
                v = c + WIRE * h
                grad = jnp.concatenate(
                    [grad_ref[v, pl.ds(2 * n, 1), :], grad_ref[v, pl.ds(2 * n + 1, 1), :]], axis=1
                )
                rows.append(jnp.where(mine, grad, 0.0))
        heads, tails = split(jnp.concatenate(rows, axis=0), 2)
        spread_ref[...] += dot_nt(
            jnp.concatenate([heads, tails], axis=1), jnp.concatenate([hot, hot], axis=1)
        )
        return carry

    lax.fori_loop(0, ROWS // 2, spread, 0)
    for c in range(WIRE):
        out_ref[pl.ds(c, DEVS, stride=WIRE), :] = spread_ref[c * 128 : (c + 1) * 128, :].T


def vmem():
    return pl.BlockSpec(memory_space=pltpu.VMEM)


def hbm():
    return pl.BlockSpec(memory_space=pltpu.HBM)


def smem():
    return pl.BlockSpec(memory_space=pltpu.SMEM)


def call(kernel, name, in_specs, outs, scratch, limit):
    return pl.pallas_call(
        kernel,
        name=name,
        out_shape=outs,
        in_specs=in_specs,
        out_specs=jax.tree.map(lambda _: vmem(), outs),
        scratch_shapes=scratch,
        compiler_params=pltpu.CompilerParams(vmem_limit_bytes=limit),
    )


def exchange(x):
    width = x.shape[0] * x.shape[1] // DEVS
    moved = lax.all_to_all(x.reshape(DEVS, 1, width), AXES, split_axis=0, concat_axis=0, tiled=True)
    return moved.reshape(x.shape)


def body(splat_params, list_owner, list_slot, list_length, target):
    shape = jax.ShapeDtypeStruct
    wire = shape((DEVS * WIRE, 128), F32)
    route = call(
        route_kernel, "route", [smem(), vmem(), vmem()],
        (shape((DEVS, 128), jnp.int32), shape((ROWS, SEGS), F32), shape((ROWS, SEGS), F32)), [], 32 << 20,
    )
    request, owners, ranks = route(list_length, list_owner.reshape(ROWS, SEGS), list_slot)
    asked = exchange(request)
    rows = splat_params.shape[1] // 8
    step = 1024
    packed = pl.pallas_call(
        pack_kernel,
        name="pack",
        grid=(rows // step,),
        out_shape=shape((rows, 128), F32),
        in_specs=[pl.BlockSpec((10, step), lambda i, g=g: (0, g * (rows // step) + i)) for g in range(8)],
        out_specs=pl.BlockSpec((step, 128), lambda i: (i, 0)),
        compiler_params=pltpu.CompilerParams(vmem_limit_bytes=61 << 20),
    )(*[splat_params] * 8)
    staging = [
        pltpu.VMEM((DEVS, 128), jnp.int32), pltpu.SMEM((DEVS, 128), jnp.int32),
        pltpu.VMEM((DEVS // BLOCK * RANKS, DEVS), BF16), pltpu.VMEM((DEVS, BLOCK * 128), BF16),
        pltpu.VMEM((BLOCK * RANKS, 128), F32),
    ]
    table = pltpu.VMEM((rows, 128), F32)
    sems = pltpu.SemaphoreType.DMA((2,))
    gather = call(gather_kernel, "gather", [vmem(), hbm()], wire, staging + [table, sems], 60 << 20)
    replies = exchange(gather(asked, packed))
    field = pltpu.VMEM((256, SEGS), F32)
    deep = pltpu.VMEM((STEPS, 256, SEGS), F32)
    render = call(
        render_kernel, "render", [vmem()] * 4, (shape(target.shape, F32), wire),
        [
            pltpu.VMEM((DEVS, ROWS * SEGS), BF16), pltpu.VMEM((WIRE * 128, 384), BF16),
            pltpu.VMEM((10, ROWS, SEGS), F32), deep, deep, pltpu.VMEM((4, 256, SEGS), F32), field, field, field,
            pltpu.VMEM((4, 256, SEGS), F32), field, field,
            pltpu.VMEM((STEPS, 16, SEGS), F32), pltpu.VMEM((STEPS, 16, SEGS), F32),
            pltpu.VMEM((10, ROWS, SEGS), F32), pltpu.VMEM((WIRE * 128, DEVS), F32),
        ],
        40 << 20,
    )
    images, outgoing = render(replies, owners, ranks, target)
    incoming = exchange(outgoing)
    scatter = pl.pallas_call(
        scatter_kernel,
        name="scatter",
        out_shape=shape(splat_params.shape, F32),
        in_specs=[vmem(), vmem()],
        out_specs=hbm(),
        scratch_shapes=staging
        + [pltpu.VMEM((128, 128), F32), pltpu.VMEM(splat_params.shape, F32), sems]
        + [table] * CHAINS,
        compiler_params=pltpu.CompilerParams(vmem_limit_bytes=48 << 20),
    )
    return (images, scatter(asked, incoming))


def solution(mesh):
    in_specs = (
        P(None, AXES),
        P(AXES, None, None),
        P(AXES, None),
        P(AXES),
        P(None, AXES, None),
    )
    out_specs = (P(None, AXES, None), P(None, AXES))
    return jax.shard_map(body, mesh=mesh, in_specs=in_specs, out_specs=out_specs, check_vma=False)
```

profile of v0, /device:TPU:1, one launch (start us, length us, event | category | flops | bytes accessed | tf_op | source)
XLA Modules:
  0.0 120.1 jit_solution(729981808766626680)
XLA Ops:
  0.6 0.0 copy-start.3
  0.6 0.7 copy-done.3
  1.3 0.0 copy-start.4
  1.4 0.7 copy-done.4
  2.1 0.0 copy-start.5
  2.1 0.7 copy-done.5
  2.7 3.2 %route.1 = (s32[128,128]{1,0:T(8,128)}, f32[32,128]{1,0:T(8,128)S(1)}, f32[32,128]{1,0:T(8,128)S(1)}) custom-call(s32[4]{0:T(128)S(1)} %copy-done.5, s32[32,128]{1,0:T(8,128)S(1)} %bitcast.14, s32[4,1024]{1,0:T(4,128)S(1)} %copy-done.4), custom_call_target="tpu_custom_call" | custom-call | tf_op jit(solution)/shard_map/route/pallas_call | solution.py:509
  5.9 11.5 %all-to-all-start = ((s32[128,1,128]{2,1,0:T(1,128)}), s32[128,1,128]{2,1,0:T(1,128)S(1)}, u32[]{:S(2)}, u32[]{:S(2)}) async-start(s32[128,1,128]{2,1,0:T(1,128)} %bitcast.2), calls=%async_computation | async-start | bytes 131072 | tf_op jit(solution)/shard_map/all_to_all | solution.py:498
  17.4 7.2 %pack.1.table_hbm = f32[8192,128]{1,0:T(8,128)} custom-call(f32[10,65536]{1,0:T(8,128)} %refs_7_.1, f32[10,65536]{1,0:T(8,128)} %refs_7_.1, f32[10,65536]{1,0:T(8,128)} %refs_7_.1, f32[10,65536]{1,0:T(8,128)} %refs_7_.1, f32[10,65536]{1,0:T(8,128)} %refs_7_.1, f32[10,65536]{1,0:T(8,128)} %refs_7_.1, f32[10,65536]{1,0:T(8,128)} %refs_7_.1, f32[10,65536]{1,0:T(8,128)} %refs_7_.1), custom_call_target="tpu_custom_call" | custom-call | tf_op jit(solution)/shard_map/pack/pallas_call | solution.py:513
  24.6 0.0 copy-start.2
  24.6 2.4 %all-to-all-done = s32[128,1,128]{2,1,0:T(1,128)S(1)} async-done(((s32[128,1,128]{2,1,0:T(1,128)}), s32[128,1,128]{2,1,0:T(1,128)S(1)}, u32[]{:S(2)}, u32[]{:S(2)}) %all-to-all-start) | async-done | bytes 65568 | tf_op jit(solution)/shard_map/all_to_all | solution.py:498
  27.0 0.0 copy-start
  27.0 0.6 copy-done
  27.7 15.7 %gather.1 = f32[640,128]{1,0:T(8,128)} custom-call(s32[128,128]{1,0:T(8,128)} %bitcast.11, f32[8192,128]{1,0:T(8,128)} %pack.1.table_hbm), custom_call_target="tpu_custom_call" | custom-call | tf_op jit(solution)/shard_map/gather/pallas_call | solution.py:530
  43.3 19.9 %all_to_all.15 = f32[128,1,640]{2,1,0:T(1,128)S(1)} all-to-all(f32[128,1,640]{2,1,0:T(1,128)} %bitcast.15), channel_id=1, replica_groups=mesh['row'=4,'col'=32] {'row','col'}, dimensions={0} | all-to-all | bytes 655360 | tf_op jit(solution)/shard_map/all_to_all | solution.py:498
  63.3 0.0 copy-done.2
  63.3 22.9 %render.1 = (f32[4,4,256]{2,1,0:T(4,128)}, f32[640,128]{1,0:T(8,128)S(1)}) custom-call(f32[640,128]{1,0:T(8,128)S(1)} %bitcast.10, f32[32,128]{1,0:T(8,128)S(1)} %get-tuple-element.8.owner_ref, f32[32,128]{1,0:T(8,128)S(1)} %get-tuple-element.9.rank_ref, f32[4,4,256]{2,1,0:T(4,128)S(1)} %copy-done.2), custom_call_target="tpu_custom_call" | custom-call | tf_op jit(solution)/shard_map/render/pallas_call | solution.py:544
  86.2 15.9 %all_to_all.16 = f32[128,1,640]{2,1,0:T(1,128)S(1)} all-to-all(f32[128,1,640]{2,1,0:T(1,128)S(1)} %bitcast.13), channel_id=1, replica_groups=mesh['row'=4,'col'=32] {'row','col'}, dimensions={0} | all-to-all | bytes 655360 | tf_op jit(solution)/shard_map/all_to_all | solution.py:498
  102.0 0.0 copy-start.1
  102.0 0.8 copy-done.1
  102.9 17.2 %scatter.1 = f32[10,65536]{1,0:T(8,128)} custom-call(s32[128,128]{1,0:T(8,128)S(1)} %bitcast.12, f32[640,128]{1,0:T(8,128)S(1)} %bitcast.9), custom_call_target="tpu_custom_call" | custom-call | tf_op jit(solution)/shard_map/scatter/pallas_call | solution.py:557
Async XLA Ops:
  0.6 0.7 copy-start.3
  1.3 0.7 copy-start.4
  2.1 0.7 copy-start.5
  5.9 21.1 %all-to-all-start = ((s32[128,1,128]{2,1,0:T(1,128)}), s32[128,1,128]{2,1,0:T(1,128)S(1)}, u32[]{:S(2)}, u32[]{:S(2)}) async-start(s32[128,1,128]{2,1,0:T(1,128)} %bitcast.2), calls=%async_computation | async-start | bytes 131072 | tf_op jit(solution)/shard_map/all_to_all | solution.py:498
  24.6 38.6 %copy-start.2 = (f32[4,4,256]{2,1,0:T(4,128)S(1)}, f32[4,4,256]{2,1,0:T(4,128)}, u32[]{:S(2)}) copy-start(f32[4,4,256]{2,1,0:T(4,128)} %target_ref.1) | copy-start | bytes 49156
  27.0 0.6 copy-start
  102.0 0.8 copy-start.1
where the time goes:
time: 121 us; the launch traced here: 120 us
  Pallas kernels  66.2 us (55%)
  blocking collectives  35.8 us (30%)
  starting transfers between devices  11.5 us (10%)
  local copies, waits for them, and re-layouts  3.54 us (3%)
  waiting for transfers between devices  2.42 us (2%)
    all_to_all x2, blocking collectives, exchange(): lax.all_to_all(x.reshape(DEVS, 1, width), AXES, split_axis=0, concat_axis...  35.8 us
    pallas_call x1, Pallas kernels, body(): images, outgoing = render(replies, owners, ranks, target)  22.9 us
    pallas_call x1, Pallas kernels, body(): return (images, scatter(asked, incoming))  17.2 us
    pallas_call x1, Pallas kernels, body(): replies = exchange(gather(asked, packed))  15.7 us
    all_to_all x1, starting transfers between devices, exchange(): lax.all_to_all(x.reshape(DEVS, 1, width), AXES, split_axis=0, concat_axis...  11.5 us
    pallas_call x1, Pallas kernels, body(): pl.pallas_call(pack_kernel, name='pack', grid=(rows // step,), out_shape=...  7.19 us
    unnamed x12, local copies, waits for them, and re-layouts  3.54 us
    pallas_call x1, Pallas kernels, body(): route(list_length, list_owner.reshape(ROWS, SEGS), list_slot)  3.21 us
  transfers between devices with their start and end apart: 1, of which 1 were waited for; matrix products, arithmetic and copies ran while one was open for 0% of the time, Pallas kernels for 6%

commit v1 on v0

--- a/solution.py
+++ b/solution.py
@@ -140,7 +140,7 @@
     return xs
 
 
-def prepare(asked_ref, table_rows, row_number_ref, number_ref, number_sem, group_ref, widen_ref):
+def prepare(asked_ref, table_rows, row_number_ref, number_ref, number_sem, group_ref):
     asked = asked_ref[...]
     lane = iota((DEVS, 128), 1)
     row_number_ref[...] = jnp.where(lane < RANKS, asked & (table_rows - 1), asked)
@@ -150,9 +150,12 @@
     for b in range(DEVS // BLOCK):
         turned = groups if b == 0 else pltpu.roll(groups, DEVS - b * BLOCK, 1)
         group_ref[b * RANKS : (b + 1) * RANKS, :] = turned.astype(BF16)
+    return copy
+
+
+def fill_widen(widen_ref):
     for n in range(BLOCK):
         widen_ref[:, n * 128 : (n + 1) * 128] = (iota((DEVS, 128), 0) == n).astype(F32).astype(BF16)
-    return copy
 
 
 def wide_groups(group_ref, widen_ref, b):
@@ -161,12 +164,13 @@
 
 
 def gather_kernel(
-    asked_ref, table_hbm, out_ref, row_number_ref, number_ref, group_ref, widen_ref, row_ref, table_ref, sems
+    asked_ref, table_hbm, out_ref, row_number_ref, group_ref, number_ref, widen_ref, row_ref, table_ref, sems
 ):
     left = iota((WIRE, 128), 1) < RANKS
     fill = pltpu.make_async_copy(table_hbm, table_ref, sems.at[1])
     fill.start()
-    copy = prepare(asked_ref, table_ref.shape[0], row_number_ref, number_ref, sems.at[0], group_ref, widen_ref)
+    copy = prepare(asked_ref, table_ref.shape[0], row_number_ref, number_ref, sems.at[0], group_ref)
+    fill_widen(widen_ref)
     row_ref[...] = jnp.zeros(row_ref.shape, F32)
     copy.wait()
     fill.wait()
@@ -210,12 +214,14 @@
 
 
 def scatter_kernel(
-    asked_ref, wire_ref, out_hbm, row_number_ref, number_ref, group_ref, widen_ref, row_ref,
+    row_number_ref, group_ref, wire_ref, out_hbm, number_ref, widen_ref, row_ref,
     turn_ref, out_ref, sems, *totals,
 ):
     left = iota((WIRE, 128), 1) < RANKS
     table_rows = totals[0].shape[0]
-    copy = prepare(asked_ref, table_rows, row_number_ref, number_ref, sems.at[0], group_ref, widen_ref)
+    copy = pltpu.make_async_copy(row_number_ref, number_ref, sems.at[0])
+    copy.start()
+    fill_widen(widen_ref)
     turn_ref[...] = jnp.zeros((128, 128), F32)
 
     def clear(i, carry):
@@ -287,32 +293,49 @@
     pltpu.make_async_copy(out_ref, out_hbm, sems.at[1]).wait()
 
 
+HALF = RANKS // 2
+KEYS = 2 * DEVS
+
+
+def marks_kernel(owner_ref, rank_ref, after_ref, hot_ref, turned_ref, mark_ref):
+    rank = rank_ref[...].astype(jnp.int32)
+    owner = owner_ref[...]
+    key = jnp.where(owner < 0.0, -1.0, owner + ((rank >> 5) * DEVS).astype(F32))
+    rest = (rank & (HALF - 1)).astype(F32)
+    columns = jnp.concatenate([key, jnp.zeros((128 - ROWS, SEGS), F32)], axis=0).T
+    for n in range(ROWS):
+        at = slice(n * SEGS, (n + 1) * SEGS)
+        hot_ref[:, at] = onehot_rows(key[n : n + 1], KEYS).astype(F32).astype(BF16)
+        mark_ref[:, at] = onehot_rows(rest[n : n + 1], HALF).astype(F32).astype(BF16)
+        column = jnp.broadcast_to(columns[:, n : n + 1], (SEGS, KEYS))
+        turned_ref[at, :] = (column == iota((SEGS, KEYS), 1).astype(F32)).astype(F32).astype(BF16)
+
+
 def render_kernel(
-    wire_ref, owner_ref, rank_ref, target_ref, image_ref, out_ref,
-    hot_ref, left_ref, value_ref, fall_ref, flow_ref, sum_ref, keep_ref, reach_ref, behind_ref,
+    wire_ref, hot_ref, turned_ref, mark_ref, target_ref, image_ref, out_ref,
+    left_ref, value_ref, fall_ref, flow_ref, sum_ref, keep_ref, reach_ref, behind_ref,
     shade_ref, column_ref, picture_ref, across_ref, tilt_ref, grad_ref, spread_ref,
 ):
     for c in range(WIRE):
         block = wire_ref[pl.ds(c, DEVS, stride=WIRE), :].T
         parts = split(block, 3)
-        left_ref[c * 128 : (c + 1) * 128, :] = jnp.concatenate(parts, axis=1)
-    rank_of = iota((RANKS, 256), 0).astype(F32)
+        for h in range(2):
+            v = c + WIRE * h
+            for half in range(2):
+                rows = slice(h * RANKS + half * HALF, h * RANKS + (half + 1) * HALF)
+                for n in range(3):
+                    at = n * KEYS + half * DEVS
+                    left_ref[v * HALF : (v + 1) * HALF, at : at + DEVS] = parts[n][rows]
 
     def fetch(n, carry):
         at = pl.ds(pl.multiple_of(n * 256, 256), 256)
-        owner = jnp.concatenate([owner_ref[pl.ds(2 * n, 1), :], owner_ref[pl.ds(2 * n + 1, 1), :]], axis=1)
-        rank = jnp.concatenate([rank_ref[pl.ds(2 * n, 1), :], rank_ref[pl.ds(2 * n + 1, 1), :]], axis=1)
-        hot = onehot_rows(owner, DEVS).astype(F32).astype(BF16)
-        hot_ref[:, at] = hot
-        mine = rank_of == rank
+        hot = hot_ref[:, at]
+        mark = mark_ref[:, at].astype(F32)
         found = dot(left_ref[...], jnp.concatenate([hot, hot, hot], axis=0))
-        for c in range(WIRE):
-            for h in range(2):
-                block = found[c * 128 + h * RANKS : c * 128 + (h + 1) * RANKS]
-                got = jnp.sum(jnp.where(mine, block, 0.0), axis=0, keepdims=True)
-                v = c + WIRE * h
-                value_ref[v, pl.ds(2 * n, 1), :] = got[:, :SEGS]
-                value_ref[v, pl.ds(2 * n + 1, 1), :] = got[:, SEGS:]
+        for v in range(10):
+            got = jnp.sum(found[v * HALF : (v + 1) * HALF] * mark, axis=0, keepdims=True)
+            value_ref[v, pl.ds(2 * n, 1), :] = got[:, :SEGS]
+            value_ref[v, pl.ds(2 * n + 1, 1), :] = got[:, SEGS:]
         return carry
 
     lax.fori_loop(0, ROWS // 2, fetch, 0)
@@ -443,30 +466,30 @@
     for ch in range(4):
         image_ref[ch] = picture[ch * TILES : (ch + 1) * TILES, :]
 
-    spread_ref[...] = jnp.zeros((WIRE * 128, DEVS), F32)
+    spread_ref[...] = jnp.zeros((10 * HALF, KEYS), F32)
 
     def spread(n, carry):
-        at = pl.ds(pl.multiple_of(n * 256, 256), 256)
-        rank = jnp.concatenate([rank_ref[pl.ds(2 * n, 1), :], rank_ref[pl.ds(2 * n + 1, 1), :]], axis=1)
-        mine = rank_of == rank
-        hot = hot_ref[:, at]
+        at = pl.ds(pl.multiple_of(n * 512, 512), 512)
+        mark = mark_ref[:, at].astype(F32)
+        heads, tails = [], []
+        for v in range(10):
+            grad = jnp.concatenate([grad_ref[v, pl.ds(4 * n + i, 1), :] for i in range(4)], axis=1)
+            head, tail = split(grad * mark, 2)
+            heads.append(head)
+            tails.append(tail)
+        turned = turned_ref[at, :]
+        both = jnp.concatenate([jnp.concatenate(heads, axis=0), jnp.concatenate(tails, axis=0)], axis=1)
+        spread_ref[...] += dot(both, jnp.concatenate([turned, turned], axis=0))
+        return carry
+
+    lax.fori_loop(0, ROWS // 4, spread, 0)
+    for c in range(WIRE):
         rows = []
-        for c in range(WIRE):
-            for h in range(2):
+        for h in range(2):
+            for half in range(2):
                 v = c + WIRE * h
-                grad = jnp.concatenate(
-                    [grad_ref[v, pl.ds(2 * n, 1), :], grad_ref[v, pl.ds(2 * n + 1, 1), :]], axis=1
-                )
-                rows.append(jnp.where(mine, grad, 0.0))
-        heads, tails = split(jnp.concatenate(rows, axis=0), 2)
-        spread_ref[...] += dot_nt(
-            jnp.concatenate([heads, tails], axis=1), jnp.concatenate([hot, hot], axis=1)
-        )
-        return carry
-
-    lax.fori_loop(0, ROWS // 2, spread, 0)
-    for c in range(WIRE):
-        out_ref[pl.ds(c, DEVS, stride=WIRE), :] = spread_ref[c * 128 : (c + 1) * 128, :].T
+                rows.append(spread_ref[v * HALF : (v + 1) * HALF, half * DEVS : (half + 1) * DEVS])
+        out_ref[pl.ds(c, DEVS, stride=WIRE), :] = jnp.concatenate(rows, axis=0).T
 
 
 def vmem():
@@ -520,41 +543,49 @@
         compiler_params=pltpu.CompilerParams(vmem_limit_bytes=61 << 20),
     )(*[splat_params] * 8)
     staging = [
-        pltpu.VMEM((DEVS, 128), jnp.int32), pltpu.SMEM((DEVS, 128), jnp.int32),
-        pltpu.VMEM((DEVS // BLOCK * RANKS, DEVS), BF16), pltpu.VMEM((DEVS, BLOCK * 128), BF16),
+        pltpu.SMEM((DEVS, 128), jnp.int32), pltpu.VMEM((DEVS, BLOCK * 128), BF16),
         pltpu.VMEM((BLOCK * RANKS, 128), F32),
     ]
     table = pltpu.VMEM((rows, 128), F32)
     sems = pltpu.SemaphoreType.DMA((2,))
-    gather = call(gather_kernel, "gather", [vmem(), hbm()], wire, staging + [table, sems], 60 << 20)
-    replies = exchange(gather(asked, packed))
+    numbers = shape((DEVS, 128), jnp.int32)
+    groups = shape((DEVS // BLOCK * RANKS, DEVS), BF16)
+    gather = call(gather_kernel, "gather", [vmem(), hbm()], (wire, numbers, groups), staging + [table, sems], 60 << 20)
+    found, numbers, groups = gather(asked, packed)
+    replies = exchange(found)
+    entries = ROWS * SEGS
+    marks = call(
+        marks_kernel, "marks", [vmem(), vmem(), hbm()],
+        (shape((KEYS, entries), BF16), shape((entries, KEYS), BF16), shape((HALF, entries), BF16)), [], 16 << 20,
+    )
+    hot, turned, mark = marks(owners, ranks, numbers)
     field = pltpu.VMEM((256, SEGS), F32)
     deep = pltpu.VMEM((STEPS, 256, SEGS), F32)
     render = call(
-        render_kernel, "render", [vmem()] * 4, (shape(target.shape, F32), wire),
+        render_kernel, "render", [vmem()] * 5, (shape(target.shape, F32), wire),
         [
-            pltpu.VMEM((DEVS, ROWS * SEGS), BF16), pltpu.VMEM((WIRE * 128, 384), BF16),
+            pltpu.VMEM((10 * HALF, 3 * KEYS), BF16),
             pltpu.VMEM((10, ROWS, SEGS), F32), deep, deep, pltpu.VMEM((4, 256, SEGS), F32), field, field, field,
             pltpu.VMEM((4, 256, SEGS), F32), field, field,
             pltpu.VMEM((STEPS, 16, SEGS), F32), pltpu.VMEM((STEPS, 16, SEGS), F32),
-            pltpu.VMEM((10, ROWS, SEGS), F32), pltpu.VMEM((WIRE * 128, DEVS), F32),
+            pltpu.VMEM((10, ROWS, SEGS), F32), pltpu.VMEM((10 * HALF, KEYS), F32),
         ],
-        40 << 20,
+        20 << 20,
     )
-    images, outgoing = render(replies, owners, ranks, target)
+    images, outgoing = render(replies, hot, turned, mark, target)
     incoming = exchange(outgoing)
     scatter = pl.pallas_call(
         scatter_kernel,
         name="scatter",
         out_shape=shape(splat_params.shape, F32),
-        in_specs=[vmem(), vmem()],
+        in_specs=[vmem(), vmem(), vmem()],
         out_specs=hbm(),
         scratch_shapes=staging
         + [pltpu.VMEM((128, 128), F32), pltpu.VMEM(splat_params.shape, F32), sems]
         + [table] * CHAINS,
         compiler_params=pltpu.CompilerParams(vmem_limit_bytes=48 << 20),
     )
-    return (images, scatter(asked, incoming))
+    return (images, scatter(numbers, groups, incoming))
 
 
 def solution(mesh):

time: 121 us -> 118 us (0.975)
  blocking collectives: 35.8 us -> 15.9 us
  starting transfers between devices: 11.5 us -> 20.5 us
  waiting for transfers between devices: 2.42 us -> 10.4 us
  Pallas kernels: 66.2 us -> 62.7 us
  local copies, waits for them, and re-layouts: 3.54 us -> 6.44 us
    all_to_all x2 -> x1, blocking collectives: 35.8 us -> 15.9 us  [exchange(): lax.all_to_all(x.reshape(DEVS, 1, width), AXES, split_axis=0, concat_axis...]
    all_to_all x1 -> x2, starting transfers between devices: 11.5 us -> 20.5 us  [exchange(): lax.all_to_all(x.reshape(DEVS, 1, width), AXES, split_axis=0, concat_axis...]
    all_to_all x1 -> x2, waiting for transfers between devices: 2.42 us -> 10.4 us  [exchange(): lax.all_to_all(x.reshape(DEVS, 1, width), AXES, split_axis=0, concat_axis...]
    pallas_call x3 -> x4, Pallas kernels: 55.8 us -> 52.3 us  [the longest x1 19.6 us: body(): images, outgoing = render(replies, hot, turned, mark, target)]
    unnamed x12 -> x20, local copies, waits for them, and re-layouts: 3.54 us -> 6.44 us
  transfers between devices with their start and end apart: 1 -> 2, of which waited for: 1 -> 2; matrix products, arithmetic and copies ran while one was open for 0% -> 0% of each run, Pallas kernels for 6% -> 7%
where the time goes in v1:
time: 118 us; the launch traced here: 117 us
  Pallas kernels  62.7 us (53%)
  starting transfers between devices  20.5 us (17%)
  blocking collectives  15.9 us (13%)
  waiting for transfers between devices  10.4 us (9%)
  local copies, waits for them, and re-layouts  6.44 us (5%)
    all_to_all x2, starting transfers between devices, exchange(): lax.all_to_all(x.reshape(DEVS, 1, width), AXES, split_axis=0, concat_axis...  20.5 us
    pallas_call x1, Pallas kernels, body(): images, outgoing = render(replies, hot, turned, mark, target)  19.6 us
    pallas_call x1, Pallas kernels, body(): return (images, scatter(numbers, groups, incoming))  16.4 us
    all_to_all x1, blocking collectives, exchange(): lax.all_to_all(x.reshape(DEVS, 1, width), AXES, split_axis=0, concat_axis...  15.9 us
    pallas_call x1, Pallas kernels, body(): found, numbers, groups = gather(asked, packed)  14.9 us
    all_to_all x2, waiting for transfers between devices, exchange(): lax.all_to_all(x.reshape(DEVS, 1, width), AXES, split_axis=0, concat_axis...  10.4 us
    pallas_call x1, Pallas kernels, body(): pl.pallas_call(pack_kernel, name='pack', grid=(rows // step,), out_shape=...  7.19 us
    unnamed x20, local copies, waits for them, and re-layouts  6.44 us
  transfers between devices with their start and end apart: 2, of which 2 were waited for; matrix products, arithmetic and copies ran while one was open for 0% of the time, Pallas kernels for 7%

profile of v1, /device:TPU:1, one launch (start us, length us, event | category | flops | bytes accessed | tf_op | source)
XLA Modules:
  0.0 116.6 jit_solution(5075273662163047779)
XLA Ops:
  0.6 0.0 copy-start.6
  0.6 0.7 copy-done.6
  1.4 0.7 copy-done.7
  2.1 0.7 copy-done.8
  2.7 3.2 %route.1 = (s32[128,128]{1,0:T(8,128)}, f32[32,128]{1,0:T(8,128)S(1)}, f32[32,128]{1,0:T(8,128)S(1)}) custom-call(s32[4]{0:T(128)S(1)} %copy-done.8, s32[32,128]{1,0:T(8,128)S(1)} %bitcast.12, s32[4,1024]{1,0:T(4,128)S(1)} %copy-done.7), custom_call_target="tpu_custom_call" | custom-call | tf_op jit(solution)/shard_map/route/pallas_call | solution.py:532
  6.0 11.5 %all-to-all-start = ((s32[128,1,128]{2,1,0:T(1,128)}), s32[128,1,128]{2,1,0:T(1,128)S(1)}, u32[]{:S(2)}, u32[]{:S(2)}) async-start(s32[128,1,128]{2,1,0:T(1,128)} %bitcast.2), calls=%async_computation | async-start | bytes 131072 | tf_op jit(solution)/shard_map/all_to_all | solution.py:521
  17.4 7.2 %pack.1.table_hbm = f32[8192,128]{1,0:T(8,128)} custom-call(f32[10,65536]{1,0:T(8,128)} %refs_7_.1, f32[10,65536]{1,0:T(8,128)} %refs_7_.1, f32[10,65536]{1,0:T(8,128)} %refs_7_.1, f32[10,65536]{1,0:T(8,128)} %refs_7_.1, f32[10,65536]{1,0:T(8,128)} %refs_7_.1, f32[10,65536]{1,0:T(8,128)} %refs_7_.1, f32[10,65536]{1,0:T(8,128)} %refs_7_.1, f32[10,65536]{1,0:T(8,128)} %refs_7_.1), custom_call_target="tpu_custom_call" | custom-call | tf_op jit(solution)/shard_map/pack/pallas_call | solution.py:536
  24.6 2.4 %all-to-all-done = s32[128,1,128]{2,1,0:T(1,128)S(1)} async-done(((s32[128,1,128]{2,1,0:T(1,128)}), s32[128,1,128]{2,1,0:T(1,128)S(1)}, u32[]{:S(2)}, u32[]{:S(2)}) %all-to-all-start) | async-done | bytes 65568 | tf_op jit(solution)/shard_map/all_to_all | solution.py:521
  27.1 0.6 copy-done.9
  27.7 14.9 %gather.1 = (f32[640,128]{1,0:T(8,128)}, s32[128,128]{1,0:T(8,128)}, bf16[512,128]{1,0:T(8,128)(2,1)}) custom-call(s32[128,128]{1,0:T(8,128)} %bitcast.14, f32[8192,128]{1,0:T(8,128)} %pack.1.table_hbm), custom_call_target="tpu_custom_call" | custom-call | tf_op jit(solution)/shard_map/gather/pallas_call | solution.py:554
  42.6 0.0 copy-start.3
  42.6 9.1 %all-to-all-start.1 = ((f32[128,1,640]{2,1,0:T(1,128)}), f32[128,1,640]{2,1,0:T(1,128)S(1)}, u32[]{:S(2)}, u32[]{:S(2)}) async-start(f32[128,1,640]{2,1,0:T(1,128)} %bitcast.13), calls=%async_computation.1 | async-start | bytes 655360 | tf_op jit(solution)/shard_map/all_to_all | solution.py:521
  51.6 0.0 copy-start.2
  51.7 0.8 copy-done.2
  52.5 1.4 %marks.1 = (bf16[256,4096]{1,0:T(8,128)(2,1)S(1)}, bf16[4096,256]{1,0:T(8,128)(2,1)S(1)}, bf16[32,4096]{1,0:T(8,128)(2,1)S(1)}) custom-call(f32[32,128]{1,0:T(8,128)S(1)} %get-tuple-element.15.owner_ref, f32[32,128]{1,0:T(8,128)S(1)} %get-tuple-element.16.rank_ref, s32[128,128]{1,0:T(8,128)S(1)} %copy-done.2), custom_call_target="tpu_custom_call" | custom-call | tf_op jit(solution)/shard_map/marks/pallas_call | solution.py:561
  53.9 0.0 copy-start
  53.9 1.3 %copy-done = bf16[4096,256]{1,0:T(8,128)(2,1)} copy-done((bf16[4096,256]{1,0:T(8,128)(2,1)}, bf16[4096,256]{1,0:T(8,128)(2,1)S(1)}, u32[]{:S(2)}) %copy-start) | copy-done | bytes 2097176
  55.3 8.0 %all-to-all-done.1 = f32[128,1,640]{2,1,0:T(1,128)S(1)} async-done(((f32[128,1,640]{2,1,0:T(1,128)}), f32[128,1,640]{2,1,0:T(1,128)S(1)}, u32[]{:S(2)}, u32[]{:S(2)}) %all-to-all-start.1) | async-done | bytes 327712 | tf_op jit(solution)/shard_map/all_to_all | solution.py:521
  63.2 0.0 copy-done.5
  63.2 1.6 %copy-done.1 = bf16[4096,256]{1,0:T(8,128)(2,1)S(1)} copy-done((bf16[4096,256]{1,0:T(8,128)(2,1)S(1)}, bf16[4096,256]{1,0:T(8,128)(2,1)}, u32[]{:S(2)}) %copy-start.1) | copy-done | bytes 2097176
  64.8 19.6 %render.1 = (f32[4,4,256]{2,1,0:T(4,128)}, f32[640,128]{1,0:T(8,128)S(1)}) custom-call(f32[640,128]{1,0:T(8,128)S(1)} %bitcast.9, bf16[256,4096]{1,0:T(8,128)(2,1)S(1)} %get-tuple-element.18.hot_ref, bf16[4096,256]{1,0:T(8,128)(2,1)S(1)} %copy-done.1, bf16[32,4096]{1,0:T(8,128)(2,1)S(1)} %get-tuple-element.20.mark_ref, f32[4,4,256]{2,1,0:T(4,128)S(1)} %copy-done.5), custom_call_target="tpu_custom_call" | custom-call | tf_op jit(solution)/shard_map/render/pallas_call | solution.py:575
  84.4 15.9 %all_to_all.15 = f32[128,1,640]{2,1,0:T(1,128)S(1)} all-to-all(f32[128,1,640]{2,1,0:T(1,128)S(1)} %bitcast.11), channel_id=1, replica_groups=mesh['row'=4,'col'=32] {'row','col'}, dimensions={0} | all-to-all | bytes 655360 | tf_op jit(solution)/shard_map/all_to_all | solution.py:521
  100.2 0.0 copy-done.3
  100.3 16.4 %scatter.1 = f32[10,65536]{1,0:T(8,128)} custom-call(s32[128,128]{1,0:T(8,128)S(1)} %copy-done.3, bf16[512,128]{1,0:T(8,128)(2,1)S(1)} %copy-done.4, f32[640,128]{1,0:T(8,128)S(1)} %bitcast.10), custom_call_target="tpu_custom_call" | custom-call | tf_op jit(solution)/shard_map/scatter/pallas_call | solution.py:588
  (7 shorter events, 0.0 us)
Async XLA Ops:
  0.6 0.7 copy-start.6
  1.3 0.7 copy-start.7
  2.1 0.7 copy-start.8
  6.0 21.1 %all-to-all-start = ((s32[128,1,128]{2,1,0:T(1,128)}), s32[128,1,128]{2,1,0:T(1,128)S(1)}, u32[]{:S(2)}, u32[]{:S(2)}) async-start(s32[128,1,128]{2,1,0:T(1,128)} %bitcast.2), calls=%async_computation | async-start | bytes 131072 | tf_op jit(solution)/shard_map/all_to_all | solution.py:521
  24.6 38.6 %copy-start.5 = (f32[4,4,256]{2,1,0:T(4,128)S(1)}, f32[4,4,256]{2,1,0:T(4,128)}, u32[]{:S(2)}) copy-start(f32[4,4,256]{2,1,0:T(4,128)} %target_ref.1) | copy-start | bytes 49156
  27.1 0.6 copy-start.9
  42.6 57.7 %copy-start.3 = (s32[128,128]{1,0:T(8,128)S(1)}, s32[128,128]{1,0:T(8,128)}, u32[]{:S(2)}) copy-start(s32[128,128]{1,0:T(8,128)} %get-tuple-element.17.after_ref.row_number_ref) | copy-start | bytes 196612
  42.6 57.7 %copy-start.4 = (bf16[512,128]{1,0:T(8,128)(2,1)S(1)}, bf16[512,128]{1,0:T(8,128)(2,1)}, u32[]{:S(2)}) copy-start(bf16[512,128]{1,0:T(8,128)(2,1)} %get-tuple-element.22.group_ref) | copy-start | bytes 393220
  42.6 20.6 %all-to-all-start.1 = ((f32[128,1,640]{2,1,0:T(1,128)}), f32[128,1,640]{2,1,0:T(1,128)S(1)}, u32[]{:S(2)}, u32[]{:S(2)}) async-start(f32[128,1,640]{2,1,0:T(1,128)} %bitcast.13), calls=%async_computation.1 | async-start | bytes 655360 | tf_op jit(solution)/shard_map/all_to_all | solution.py:521
  51.6 0.8 copy-start.2
  53.9 1.3 %copy-start = (bf16[4096,256]{1,0:T(8,128)(2,1)}, bf16[4096,256]{1,0:T(8,128)(2,1)S(1)}, u32[]{:S(2)}) copy-start(bf16[4096,256]{1,0:T(8,128)(2,1)S(1)} %get-tuple-element.19.turned_ref) | copy-start | bytes 6291460
  63.2 1.6 %copy-start.1 = (bf16[4096,256]{1,0:T(8,128)(2,1)S(1)}, bf16[4096,256]{1,0:T(8,128)(2,1)}, u32[]{:S(2)}) copy-start(bf16[4096,256]{1,0:T(8,128)(2,1)} %copy-done) | copy-start | bytes 6291460

commit v2 on v1

--- a/solution.py
+++ b/solution.py
@@ -15,9 +15,15 @@
 WIRE = 5
 GROUP = 16
 BLOCK = 16
-CHUNKS = ((0, 32), (32, 48), (48, 64))
-CLOSE = 1024
-CHAINS = 4
+CHUNKS = ((0, 48), (48, 64))
+STRETCH = 1024
+UNROLL = 4
+SPLIT_UNROLL = 2
+FORE = 4
+FETCH = 4096
+SPREAD = 4096
+BACK = 8
+CHAINS = 8
 LOG2E = 1.4426950408889634
 F32 = jnp.float32
 BF16 = jnp.bfloat16
@@ -102,14 +108,34 @@
     request_ref[...] = full.astype(jnp.int32)
 
 
-def pack_kernel(*refs):
-    out_ref = refs[-1]
+def pack_kernel(params_hbm, out_hbm, params_ref, out_ref, in_sems, out_sem):
+    width = 8 * STRETCH
+    steps = params_ref.shape[1] // width
     pad = jnp.zeros((GROUP - 10, 128), F32)
-    for n in range(refs[0].shape[1] // 128):
-        blocks = []
-        for ref in refs[:-1]:
-            blocks += [ref[:, n * 128 : (n + 1) * 128], pad]
-        out_ref[n * 128 : (n + 1) * 128, :] = jnp.concatenate(blocks, axis=0).T
+
+    def read(i):
+        at = pl.ds(pl.multiple_of(i * width, width), width)
+        return pltpu.make_async_copy(params_hbm.at[:, at], params_ref.at[:, at], in_sems.at[i])
+
+    for i in range(steps):
+        read(i).start()
+
+    def step(i, carry):
+        read(i).wait()
+        mine_ref = params_ref.at[:, pl.ds(pl.multiple_of(i * width, width), width)]
+        rows = pl.ds(pl.multiple_of(i * STRETCH, STRETCH), STRETCH)
+        done_ref = out_ref.at[rows]
+        for n in range(STRETCH // 128):
+            blocks = []
+            for g in range(8):
+                at = g * STRETCH + n * 128
+                blocks += [mine_ref[:, at : at + 128], pad]
+            done_ref[n * 128 : (n + 1) * 128, :] = jnp.concatenate(blocks, axis=0).T
+        pltpu.make_async_copy(done_ref, out_hbm.at[rows], out_sem).start()
+        return carry
+
+    lax.fori_loop(0, steps, step, 0)
+    pltpu.make_async_copy(out_ref, out_hbm, out_sem).wait()
 
 
 def bit_clear(shift):
@@ -140,13 +166,15 @@
     return xs
 
 
-def prepare(asked_ref, table_rows, row_number_ref, number_ref, number_sem, group_ref):
+def prepare(asked_ref, row_number_ref, number_ref, number_sem, group_ref):
     asked = asked_ref[...]
     lane = iota((DEVS, 128), 1)
-    row_number_ref[...] = jnp.where(lane < RANKS, asked & (table_rows - 1), asked)
+    row = ((asked >> 13) << 10) | (asked & (STRETCH - 1))
+    row_number_ref[...] = jnp.where(lane < RANKS, row, asked)
     copy = pltpu.make_async_copy(row_number_ref, number_ref, number_sem)
     copy.start()
-    groups = lax.div(asked, table_rows).astype(F32).T[:RANKS]
+    group = jnp.where(lane < pltpu.roll(asked, RANKS, 1), (asked >> 10) & 7, 8)
+    groups = group.astype(F32).T[:RANKS]
     for b in range(DEVS // BLOCK):
         turned = groups if b == 0 else pltpu.roll(groups, DEVS - b * BLOCK, 1)
         group_ref[b * RANKS : (b + 1) * RANKS, :] = turned.astype(BF16)
@@ -169,34 +197,34 @@
     left = iota((WIRE, 128), 1) < RANKS
     fill = pltpu.make_async_copy(table_hbm, table_ref, sems.at[1])
     fill.start()
-    copy = prepare(asked_ref, table_ref.shape[0], row_number_ref, number_ref, sems.at[0], group_ref)
+    copy = prepare(asked_ref, row_number_ref, number_ref, sems.at[0], group_ref)
     fill_widen(widen_ref)
-    row_ref[...] = jnp.zeros(row_ref.shape, F32)
     copy.wait()
     fill.wait()
 
+    def source(src, carry):
+        count = number_ref[src, RANKS]
+        mine_ref = row_ref.at[pl.ds(pl.multiple_of(src * RANKS, RANKS), RANKS)]
+        for first, last in CHUNKS:
+
+            @pl.when(count > first)
+            def _():
+                for rank in range(first, last):
+                    mine_ref[rank : rank + 1, :] = table_ref[pl.ds(number_ref[src, rank], 1), :]
+
+        return carry
+
+    lax.fori_loop(0, DEVS, source, 0)
+
     def block(b, carry):
-        def source(q, carry):
-            src = b * BLOCK + q
-            count = number_ref[src, RANKS]
-            mine_ref = row_ref.at[pl.ds(pl.multiple_of(q * RANKS, RANKS), RANKS)]
-            for first, last in CHUNKS:
-
-                @pl.when(count > first)
-                def _():
-                    for rank in range(first, last):
-                        mine_ref[rank : rank + 1, :] = table_ref[pl.ds(number_ref[src, rank], 1), :]
-
-            return carry
-
-        lax.fori_loop(0, BLOCK, source, 0)
+        base = pl.multiple_of(b * BLOCK * RANKS, BLOCK * RANKS)
         groups = wide_groups(group_ref, widen_ref, b)
         lane_group = (iota((RANKS, 128), 1) >> 4).astype(F32)
         halves = []
         for half in range(2):
             picked = []
             for n in range(half * 8, half * 8 + 8):
-                rows = row_ref[n * RANKS : (n + 1) * RANKS, :]
+                rows = row_ref[pl.ds(base + n * RANKS, RANKS), :]
                 picked.append(jnp.where(lane_group == groups[:, n * 128 : (n + 1) * 128], rows, 0.0))
             halves.append(merge_groups(picked))
         turned = jnp.concatenate(halves, axis=0).T
@@ -210,19 +238,18 @@
         out_ref[pl.ds(at, BLOCK * WIRE), :] = jnp.concatenate(evens + odds, axis=0)
         return carry
 
-    lax.fori_loop(0, DEVS // BLOCK, block, 0)
+    lax.fori_loop(0, DEVS // BLOCK, block, 0, unroll=UNROLL)
 
 
 def scatter_kernel(
-    row_number_ref, group_ref, wire_ref, out_hbm, number_ref, widen_ref, row_ref,
-    turn_ref, out_ref, sems, *totals,
+    row_number_ref, group_ref, wire_ref, out_hbm, number_ref, widen_ref, row_ref, turn_ref, out_ref, sems, *totals
 ):
     left = iota((WIRE, 128), 1) < RANKS
     table_rows = totals[0].shape[0]
     copy = pltpu.make_async_copy(row_number_ref, number_ref, sems.at[0])
     copy.start()
     fill_widen(widen_ref)
-    turn_ref[...] = jnp.zeros((128, 128), F32)
+    turn_ref[...] = jnp.zeros(turn_ref.shape, F32)
 
     def clear(i, carry):
         for ref in totals:
@@ -230,66 +257,68 @@
         return carry
 
     lax.fori_loop(0, table_rows // 256, clear, 0)
-    copy.wait()
 
     def block(b, carry):
         at = pl.multiple_of(b * BLOCK * WIRE, 8)
+        base = pl.multiple_of(b * BLOCK * RANKS, BLOCK * RANKS)
         wire = wire_ref[pl.ds(at, BLOCK * WIRE), :]
+        mine_ref = turn_ref.at[b]
         for q in range(8):
             even = wire[q * WIRE : (q + 1) * WIRE]
             odd = wire[(q + 8) * WIRE : (q + 9) * WIRE]
-            turn_ref[q * GROUP : q * GROUP + WIRE, :] = jnp.where(left, even, pltpu.roll(odd, RANKS, 1))
-            turn_ref[q * GROUP + WIRE : q * GROUP + 2 * WIRE, :] = jnp.where(left, pltpu.roll(even, RANKS, 1), odd)
-        turned = turn_ref[...].T
+            mine_ref[q * GROUP : q * GROUP + WIRE, :] = jnp.where(left, even, pltpu.roll(odd, RANKS, 1))
+            mine_ref[q * GROUP + WIRE : q * GROUP + 2 * WIRE, :] = jnp.where(left, pltpu.roll(even, RANKS, 1), odd)
+        turned = mine_ref[...].T
         groups = wide_groups(group_ref, widen_ref, b)
         lane_group = (iota((RANKS, 128), 1) >> 4).astype(F32)
         for half in range(2):
             spreads = spread_groups(turned[half * RANKS : (half + 1) * RANKS])
             for q in range(8):
                 n = half * 8 + q
-                row_ref[n * RANKS : (n + 1) * RANKS, :] = jnp.where(
+                row_ref[pl.ds(base + n * RANKS, RANKS), :] = jnp.where(
                     lane_group == groups[:, n * 128 : (n + 1) * 128], spreads[q], 0.0
                 )
-
-        def source(q, carry):
-            src = b * BLOCK + q
-            count = number_ref[src, RANKS]
-            mine_ref = row_ref.at[pl.ds(pl.multiple_of(q * RANKS, RANKS), RANKS)]
-            for first, last in CHUNKS:
-
-                @pl.when(count > first)
-                def _():
-                    for start in range(first, last, CHAINS):
-                        news = []
-                        for i, ref in enumerate(totals):
-                            row = number_ref[src, start + i]
-                            news.append((row, mine_ref[start + i : start + i + 1, :] + ref[pl.ds(row, 1), :]))
-                        for ref, (row, total) in zip(totals, news):
-                            ref[pl.ds(row, 1), :] = total
-
-            return carry
-
-        lax.fori_loop(0, BLOCK, source, 0)
-        return carry
-
-    lax.fori_loop(0, DEVS // BLOCK, block, 0)
+        return carry
+
+    lax.fori_loop(0, DEVS // BLOCK, block, 0, unroll=SPLIT_UNROLL)
+    copy.wait()
+
+    def source(src, carry):
+        count = number_ref[src, RANKS]
+        mine_ref = row_ref.at[pl.ds(pl.multiple_of(src * RANKS, RANKS), RANKS)]
+        for first, last in CHUNKS:
+
+            @pl.when(count > first)
+            def _():
+                for start in range(first, last, CHAINS):
+                    news = []
+                    for i, ref in enumerate(totals[: last - start]):
+                        row = number_ref[src, start + i]
+                        news.append((row, mine_ref[start + i : start + i + 1, :] + ref[pl.ds(row, 1), :]))
+                    for ref, (row, total) in zip(totals, news):
+                        ref[pl.ds(row, 1), :] = total
+
+        return carry
+
+    lax.fori_loop(0, DEVS, source, 0)
 
     def close(i, carry):
-        base = pl.multiple_of(i * CLOSE, CLOSE)
-        for n in range(CLOSE // 128):
+        base = pl.multiple_of(i * STRETCH, STRETCH)
+        lanes = pl.ds(pl.multiple_of(i * 8 * STRETCH, 8 * STRETCH), 8 * STRETCH)
+        mine_ref = out_ref.at[:, lanes]
+        for n in range(STRETCH // 128):
             at = pl.ds(base + n * 128, 128)
             total = totals[0][at, :]
             for ref in totals[1:]:
                 total = total + ref[at, :]
             total = total.T
             for g in range(8):
-                out_ref[:, pl.ds(g * table_rows + base + n * 128, 128)] = total[g * GROUP : g * GROUP + 10]
-        for g in range(8):
-            lanes = pl.ds(pl.multiple_of(g * table_rows + base, CLOSE), CLOSE)
-            pltpu.make_async_copy(out_ref.at[:, lanes], out_hbm.at[:, lanes], sems.at[1]).start()
-        return carry
-
-    lax.fori_loop(0, table_rows // CLOSE, close, 0)
+                spot = g * STRETCH + n * 128
+                mine_ref[:, spot : spot + 128] = total[g * GROUP : g * GROUP + 10]
+        pltpu.make_async_copy(mine_ref, out_hbm.at[:, lanes], sems.at[1]).start()
+        return carry
+
+    lax.fori_loop(0, table_rows // STRETCH, close, 0)
     pltpu.make_async_copy(out_ref, out_hbm, sems.at[1]).wait()
 
 
@@ -297,23 +326,21 @@
 KEYS = 2 * DEVS
 
 
-def marks_kernel(owner_ref, rank_ref, after_ref, hot_ref, turned_ref, mark_ref):
+def marks_kernel(owner_ref, rank_ref, after_ref, hot_ref, mark_ref, key_ref):
     rank = rank_ref[...].astype(jnp.int32)
     owner = owner_ref[...]
     key = jnp.where(owner < 0.0, -1.0, owner + ((rank >> 5) * DEVS).astype(F32))
     rest = (rank & (HALF - 1)).astype(F32)
-    columns = jnp.concatenate([key, jnp.zeros((128 - ROWS, SEGS), F32)], axis=0).T
+    key_ref[...] = key
     for n in range(ROWS):
         at = slice(n * SEGS, (n + 1) * SEGS)
         hot_ref[:, at] = onehot_rows(key[n : n + 1], KEYS).astype(F32).astype(BF16)
         mark_ref[:, at] = onehot_rows(rest[n : n + 1], HALF).astype(F32).astype(BF16)
-        column = jnp.broadcast_to(columns[:, n : n + 1], (SEGS, KEYS))
-        turned_ref[at, :] = (column == iota((SEGS, KEYS), 1).astype(F32)).astype(F32).astype(BF16)
 
 
 def render_kernel(
-    wire_ref, hot_ref, turned_ref, mark_ref, target_ref, image_ref, out_ref,
-    left_ref, value_ref, fall_ref, flow_ref, sum_ref, keep_ref, reach_ref, behind_ref,
+    wire_ref, hot_ref, mark_ref, key_ref, target_ref, image_ref, out_ref,
+    turned_ref,    left_ref, value_ref, fall_ref, flow_ref, sum_ref, keep_ref, reach_ref, behind_ref,
     shade_ref, column_ref, picture_ref, across_ref, tilt_ref, grad_ref, spread_ref,
 ):
     for c in range(WIRE):
@@ -327,18 +354,23 @@
                     at = n * KEYS + half * DEVS
                     left_ref[v * HALF : (v + 1) * HALF, at : at + DEVS] = parts[n][rows]
 
+    columns = jnp.concatenate([key_ref[...], jnp.zeros((128 - ROWS, SEGS), F32)], axis=0).T
+    for n in range(ROWS):
+        column = jnp.broadcast_to(columns[:, n : n + 1], (SEGS, KEYS))
+        turned_ref[n * SEGS : (n + 1) * SEGS, :] = (column == iota((SEGS, KEYS), 1).astype(F32)).astype(F32).astype(BF16)
+
     def fetch(n, carry):
-        at = pl.ds(pl.multiple_of(n * 256, 256), 256)
+        at = pl.ds(pl.multiple_of(n * FETCH, FETCH), FETCH)
         hot = hot_ref[:, at]
         mark = mark_ref[:, at].astype(F32)
         found = dot(left_ref[...], jnp.concatenate([hot, hot, hot], axis=0))
         for v in range(10):
             got = jnp.sum(found[v * HALF : (v + 1) * HALF] * mark, axis=0, keepdims=True)
-            value_ref[v, pl.ds(2 * n, 1), :] = got[:, :SEGS]
-            value_ref[v, pl.ds(2 * n + 1, 1), :] = got[:, SEGS:]
-        return carry
-
-    lax.fori_loop(0, ROWS // 2, fetch, 0)
+            for i in range(FETCH // SEGS):
+                value_ref[v, pl.ds(n * (FETCH // SEGS) + i, 1), :] = got[:, i * SEGS : (i + 1) * SEGS]
+        return carry
+
+    lax.fori_loop(0, ROWS * SEGS // FETCH, fetch, 0)
 
     flat = jnp.concatenate([target_ref[ch] for ch in range(4)] + [jnp.zeros((112, 256), F32)], axis=0)
     column_ref[...] = jnp.concatenate([flat[:, :128].T, flat[:, 128:].T], axis=0)
@@ -382,7 +414,7 @@
                     sum_ref[ch, at, :] = sums[ch]
             return carry
 
-        lax.fori_loop(0, 8, forward, 0)
+        lax.fori_loop(0, 8, forward, 0, unroll=FORE)
 
         keep = keep_ref[...]
         logs = jnp.concatenate(split(jnp.log(keep), 3), axis=1)
@@ -434,7 +466,7 @@
 
             blank = jnp.zeros((8, SEGS), F32)
             zero, one, two, tints = lax.fori_loop(
-                0, 8, backward, ((blank,) * 2, (blank,) * 2, (blank,) * 2, (blank,) * 4)
+                0, 8, backward, ((blank,) * 2, (blank,) * 2, (blank,) * 2, (blank,) * 4), unroll=BACK
             )
             total = lambda x: jnp.sum(x, axis=0, keepdims=True)
             offset_x = pixel_x - value(0)
@@ -469,11 +501,12 @@
     spread_ref[...] = jnp.zeros((10 * HALF, KEYS), F32)
 
     def spread(n, carry):
-        at = pl.ds(pl.multiple_of(n * 512, 512), 512)
+        at = pl.ds(pl.multiple_of(n * SPREAD, SPREAD), SPREAD)
         mark = mark_ref[:, at].astype(F32)
         heads, tails = [], []
         for v in range(10):
-            grad = jnp.concatenate([grad_ref[v, pl.ds(4 * n + i, 1), :] for i in range(4)], axis=1)
+            count = SPREAD // SEGS
+            grad = jnp.concatenate([grad_ref[v, pl.ds(count * n + i, 1), :] for i in range(count)], axis=1)
             head, tail = split(grad * mark, 2)
             heads.append(head)
             tails.append(tail)
@@ -482,7 +515,7 @@
         spread_ref[...] += dot(both, jnp.concatenate([turned, turned], axis=0))
         return carry
 
-    lax.fori_loop(0, ROWS // 4, spread, 0)
+    lax.fori_loop(0, ROWS * SEGS // SPREAD, spread, 0)
     for c in range(WIRE):
         rows = []
         for h in range(2):
@@ -532,19 +565,21 @@
     request, owners, ranks = route(list_length, list_owner.reshape(ROWS, SEGS), list_slot)
     asked = exchange(request)
     rows = splat_params.shape[1] // 8
-    step = 1024
     packed = pl.pallas_call(
         pack_kernel,
         name="pack",
-        grid=(rows // step,),
         out_shape=shape((rows, 128), F32),
-        in_specs=[pl.BlockSpec((10, step), lambda i, g=g: (0, g * (rows // step) + i)) for g in range(8)],
-        out_specs=pl.BlockSpec((step, 128), lambda i: (i, 0)),
+        in_specs=[hbm()],
+        out_specs=hbm(),
+        scratch_shapes=[
+            pltpu.VMEM(splat_params.shape, F32), pltpu.VMEM((rows, 128), F32),
+            pltpu.SemaphoreType.DMA((rows // STRETCH,)), pltpu.SemaphoreType.DMA,
+        ],
         compiler_params=pltpu.CompilerParams(vmem_limit_bytes=61 << 20),
-    )(*[splat_params] * 8)
+    )(splat_params)
     staging = [
         pltpu.SMEM((DEVS, 128), jnp.int32), pltpu.VMEM((DEVS, BLOCK * 128), BF16),
-        pltpu.VMEM((BLOCK * RANKS, 128), F32),
+        pltpu.VMEM((DEVS * RANKS, 128), F32),
     ]
     table = pltpu.VMEM((rows, 128), F32)
     sems = pltpu.SemaphoreType.DMA((2,))
@@ -556,23 +591,23 @@
     entries = ROWS * SEGS
     marks = call(
         marks_kernel, "marks", [vmem(), vmem(), hbm()],
-        (shape((KEYS, entries), BF16), shape((entries, KEYS), BF16), shape((HALF, entries), BF16)), [], 16 << 20,
+        (shape((KEYS, entries), BF16), shape((HALF, entries), BF16), shape((ROWS, SEGS), F32)), [], 16 << 20,
     )
-    hot, turned, mark = marks(owners, ranks, numbers)
+    hot, mark, keys = marks(owners, ranks, numbers)
     field = pltpu.VMEM((256, SEGS), F32)
     deep = pltpu.VMEM((STEPS, 256, SEGS), F32)
     render = call(
         render_kernel, "render", [vmem()] * 5, (shape(target.shape, F32), wire),
         [
-            pltpu.VMEM((10 * HALF, 3 * KEYS), BF16),
+            pltpu.VMEM((entries, KEYS), BF16), pltpu.VMEM((10 * HALF, 3 * KEYS), BF16),
             pltpu.VMEM((10, ROWS, SEGS), F32), deep, deep, pltpu.VMEM((4, 256, SEGS), F32), field, field, field,
             pltpu.VMEM((4, 256, SEGS), F32), field, field,
             pltpu.VMEM((STEPS, 16, SEGS), F32), pltpu.VMEM((STEPS, 16, SEGS), F32),
             pltpu.VMEM((10, ROWS, SEGS), F32), pltpu.VMEM((10 * HALF, KEYS), F32),
         ],
-        20 << 20,
+        24 << 20,
     )
-    images, outgoing = render(replies, hot, turned, mark, target)
+    images, outgoing = render(replies, hot, mark, keys, target)
     incoming = exchange(outgoing)
     scatter = pl.pallas_call(
         scatter_kernel,
@@ -581,9 +616,9 @@
         in_specs=[vmem(), vmem(), vmem()],
         out_specs=hbm(),
         scratch_shapes=staging
-        + [pltpu.VMEM((128, 128), F32), pltpu.VMEM(splat_params.shape, F32), sems]
+        + [pltpu.VMEM((DEVS // BLOCK, 128, 128), F32), pltpu.VMEM(splat_params.shape, F32), sems]
         + [table] * CHAINS,
-        compiler_params=pltpu.CompilerParams(vmem_limit_bytes=48 << 20),
+        compiler_params=pltpu.CompilerParams(vmem_limit_bytes=56 << 20),
     )
     return (images, scatter(numbers, groups, incoming))
 

time: 118 us -> 103 us (0.87); the launches traced: 117 us -> 103 us
  Pallas kernels: 62.7 us -> 51 us
  waiting for transfers between devices: 10.4 us -> 16.1 us
  starting transfers between devices: 20.5 us -> 15.5 us
  local copies, waits for them, and re-layouts: 6.44 us -> 3.53 us
    pallas_call x3, Pallas kernels: 28.2 us -> 17.4 us  [the longest x1 13.3 us: body(): images, outgoing = render(replies, hot, mark, keys, target)]
    all_to_all x2, waiting for transfers between devices: 10.4 us -> 16.1 us  [exchange(): lax.all_to_all(x.reshape(DEVS, 1, width), AXES, split_axis=0, concat_axis...]
    all_to_all x2, starting transfers between devices: 20.5 us -> 15.5 us  [exchange(): lax.all_to_all(x.reshape(DEVS, 1, width), AXES, split_axis=0, concat_axis...]
    unnamed x20 -> x12, local copies, waits for them, and re-layouts: 6.44 us -> 3.53 us
  transfers between devices with their start and end apart: 2 -> 2, of which waited for: 2 -> 2; matrix products, arithmetic and copies ran while one was open for 0% -> 0% of each run, Pallas kernels for 7% -> 4%
where the time goes in v2:
time: 103 us
  Pallas kernels  51 us (50%)
  waiting for transfers between devices  16.1 us (16%)
  blocking collectives  16.1 us (16%)
  starting transfers between devices  15.5 us (15%)
  local copies, waits for them, and re-layouts  3.53 us (3%)
    pallas_call x1, Pallas kernels, body(): return (images, scatter(numbers, groups, incoming))  16.6 us
    all_to_all x2, waiting for transfers between devices, exchange(): lax.all_to_all(x.reshape(DEVS, 1, width), AXES, split_axis=0, concat_axis...  16.1 us
    all_to_all x1, blocking collectives, exchange(): lax.all_to_all(x.reshape(DEVS, 1, width), AXES, split_axis=0, concat_axis...  16.1 us
    all_to_all x2, starting transfers between devices, exchange(): lax.all_to_all(x.reshape(DEVS, 1, width), AXES, split_axis=0, concat_axis...  15.5 us
    pallas_call x1, Pallas kernels, body(): found, numbers, groups = gather(asked, packed)  13.8 us
    pallas_call x1, Pallas kernels, body(): images, outgoing = render(replies, hot, mark, keys, target)  13.3 us
    pallas_call x1, Pallas kernels, body(): pl.pallas_call(pack_kernel, name='pack', out_shape=shape((rows, 128), F32...  3.54 us
    unnamed x12, local copies, waits for them, and re-layouts  3.53 us
  transfers between devices with their start and end apart: 2, of which 2 were waited for; matrix products, arithmetic and copies ran while one was open for 0% of the time, Pallas kernels for 4%

profile of v2, /device:TPU:1, one launch (start us, length us, event | category | flops | bytes accessed | tf_op | source)
XLA Modules:
  0.0 103.0 jit_solution(9607191199777168184)
XLA Ops:
  0.6 0.0 copy-start.2
  0.6 0.7 copy-done.2
  1.3 0.0 copy-start.3
  1.4 0.7 copy-done.3
  2.1 0.0 copy-start.4
  2.1 0.7 copy-done.4
  2.7 3.2 %route.1 = (s32[128,128]{1,0:T(8,128)}, f32[32,128]{1,0:T(8,128)S(1)}, f32[32,128]{1,0:T(8,128)S(1)}) custom-call(s32[4]{0:T(128)S(1)} %copy-done.4, s32[32,128]{1,0:T(8,128)S(1)} %bitcast.11, s32[4,1024]{1,0:T(4,128)S(1)} %copy-done.3), custom_call_target="tpu_custom_call" | custom-call | tf_op jit(solution)/shard_map/route/pallas_call | solution.py:565
  5.9 11.5 %all-to-all-start = ((s32[128,1,128]{2,1,0:T(1,128)}), s32[128,1,128]{2,1,0:T(1,128)S(1)}, u32[]{:S(2)}, u32[]{:S(2)}) async-start(s32[128,1,128]{2,1,0:T(1,128)} %bitcast.2), calls=%async_computation | async-start | bytes 131072 | tf_op jit(solution)/shard_map/all_to_all | solution.py:554
  17.4 3.5 %pack.1.table_hbm = f32[8192,128]{1,0:T(8,128)} custom-call(f32[10,65536]{1,0:T(8,128)} %params_hbm.1), custom_call_target="tpu_custom_call" | custom-call | tf_op jit(solution)/shard_map/pack/pallas_call | solution.py:568
  21.0 0.0 copy-start.1
  21.0 6.0 %all-to-all-done = s32[128,1,128]{2,1,0:T(1,128)S(1)} async-done(((s32[128,1,128]{2,1,0:T(1,128)}), s32[128,1,128]{2,1,0:T(1,128)S(1)}, u32[]{:S(2)}, u32[]{:S(2)}) %all-to-all-start) | async-done | bytes 65568 | tf_op jit(solution)/shard_map/all_to_all | solution.py:554
  27.0 0.0 copy-start.5
  27.0 0.6 copy-done.5
  27.7 13.8 %gather.1 = (f32[640,128]{1,0:T(8,128)}, s32[128,128]{1,0:T(8,128)}, bf16[512,128]{1,0:T(8,128)(2,1)}) custom-call(s32[128,128]{1,0:T(8,128)} %bitcast.14, f32[8192,128]{1,0:T(8,128)} %pack.1.table_hbm), custom_call_target="tpu_custom_call" | custom-call | tf_op jit(solution)/shard_map/gather/pallas_call | solution.py:589
  41.4 4.1 %all-to-all-start.1 = ((f32[128,1,640]{2,1,0:T(1,128)}), f32[128,1,640]{2,1,0:T(1,128)S(1)}, u32[]{:S(2)}, u32[]{:S(2)}) async-start(f32[128,1,640]{2,1,0:T(1,128)} %bitcast.13), calls=%async_computation.1 | async-start | bytes 655360 | tf_op jit(solution)/shard_map/all_to_all | solution.py:554
  45.5 0.0 copy-start
  45.5 0.8 copy-done
  46.3 0.6 marks.1
  47.0 10.1 %all-to-all-done.1 = f32[128,1,640]{2,1,0:T(1,128)S(1)} async-done(((f32[128,1,640]{2,1,0:T(1,128)}), f32[128,1,640]{2,1,0:T(1,128)S(1)}, u32[]{:S(2)}, u32[]{:S(2)}) %all-to-all-start.1) | async-done | bytes 327712 | tf_op jit(solution)/shard_map/all_to_all | solution.py:554
  57.1 0.0 copy-done.1
  57.1 13.3 %render.1 = (f32[4,4,256]{2,1,0:T(4,128)}, f32[640,128]{1,0:T(8,128)S(1)}) custom-call(f32[640,128]{1,0:T(8,128)S(1)} %bitcast.9, bf16[256,4096]{1,0:T(8,128)(2,1)S(1)} %get-tuple-element.18.hot_ref, bf16[32,4096]{1,0:T(8,128)(2,1)S(1)} %get-tuple-element.19.mark_ref, f32[32,128]{1,0:T(8,128)S(1)} %get-tuple-element.20.key_ref, f32[4,4,256]{2,1,0:T(4,128)S(1)} %copy-done.1), custom_call_target="tpu_custom_call" | custom-call | tf_op jit(solution)/shard_map/render/pallas_call | solution.py:610
  70.3 16.1 %all_to_all.15 = f32[128,1,640]{2,1,0:T(1,128)} all-to-all(f32[128,1,640]{2,1,0:T(1,128)S(1)} %bitcast.10), channel_id=1, replica_groups=mesh['row'=4,'col'=32] {'row','col'}, dimensions={0} | all-to-all | bytes 655360 | tf_op jit(solution)/shard_map/all_to_all | solution.py:554
  86.4 16.6 %scatter.1 = f32[10,65536]{1,0:T(8,128)} custom-call(s32[128,128]{1,0:T(8,128)} %get-tuple-element.17.after_ref.row_number_ref, bf16[512,128]{1,0:T(8,128)(2,1)} %get-tuple-element.22.group_ref, f32[640,128]{1,0:T(8,128)} %bitcast.12), custom_call_target="tpu_custom_call" | custom-call | tf_op jit(solution)/shard_map/scatter/pallas_call | solution.py:623
Async XLA Ops:
  0.6 0.7 copy-start.2
  1.3 0.7 copy-start.3
  2.1 0.7 copy-start.4
  5.9 21.1 %all-to-all-start = ((s32[128,1,128]{2,1,0:T(1,128)}), s32[128,1,128]{2,1,0:T(1,128)S(1)}, u32[]{:S(2)}, u32[]{:S(2)}) async-start(s32[128,1,128]{2,1,0:T(1,128)} %bitcast.2), calls=%async_computation | async-start | bytes 131072 | tf_op jit(solution)/shard_map/all_to_all | solution.py:554
  21.0 36.1 %copy-start.1 = (f32[4,4,256]{2,1,0:T(4,128)S(1)}, f32[4,4,256]{2,1,0:T(4,128)}, u32[]{:S(2)}) copy-start(f32[4,4,256]{2,1,0:T(4,128)} %target_ref.1) | copy-start | bytes 49156
  27.0 0.6 copy-start.5
  41.4 15.6 %all-to-all-start.1 = ((f32[128,1,640]{2,1,0:T(1,128)}), f32[128,1,640]{2,1,0:T(1,128)S(1)}, u32[]{:S(2)}, u32[]{:S(2)}) async-start(f32[128,1,640]{2,1,0:T(1,128)} %bitcast.13), calls=%async_computation.1 | async-start | bytes 655360 | tf_op jit(solution)/shard_map/all_to_all | solution.py:554
  45.5 0.8 copy-start

commit v3 on v2

--- a/solution.py
+++ b/solution.py
@@ -18,12 +18,13 @@
 CHUNKS = ((0, 48), (48, 64))
 STRETCH = 1024
 UNROLL = 4
+ROUTE_LIMIT = 63 << 20
 SPLIT_UNROLL = 2
 FORE = 4
 FETCH = 4096
 SPREAD = 4096
 BACK = 8
-CHAINS = 8
+CHAINS = 6
 LOG2E = 1.4426950408889634
 F32 = jnp.float32
 BF16 = jnp.bfloat16
@@ -56,7 +57,15 @@
     return wide == iota(wide.shape, 0).astype(F32)
 
 
-def route_kernel(length_ref, owner_ref, slot_ref, request_ref, owner_out, rank_out):
+def route_kernel(
+    length_hbm, owner_hbm, slot_hbm, request_ref, owner_out, rank_out, length_ref, owner_ref, slot_ref, sems
+):
+    pairs = ((length_hbm, length_ref), (owner_hbm, owner_ref), (slot_hbm, slot_ref))
+    copies = [pltpu.make_async_copy(a, b, sems.at[i]) for i, (a, b) in enumerate(pairs)]
+    for copy in copies:
+        copy.start()
+    for copy in copies:
+        copy.wait()
     lane = iota((STEPS, SEGS), 1)
     step = iota((STEPS, SEGS), 0)
     picks = (lane & (STEPS - 1)) == step
@@ -559,8 +568,13 @@
     shape = jax.ShapeDtypeStruct
     wire = shape((DEVS * WIRE, 128), F32)
     route = call(
-        route_kernel, "route", [smem(), vmem(), vmem()],
-        (shape((DEVS, 128), jnp.int32), shape((ROWS, SEGS), F32), shape((ROWS, SEGS), F32)), [], 32 << 20,
+        route_kernel, "route", [hbm(), hbm(), hbm()],
+        (shape((DEVS, 128), jnp.int32), shape((ROWS, SEGS), F32), shape((ROWS, SEGS), F32)),
+        [
+            pltpu.SMEM(list_length.shape, jnp.int32), pltpu.VMEM((ROWS, SEGS), jnp.int32),
+            pltpu.VMEM(list_slot.shape, jnp.int32), pltpu.SemaphoreType.DMA((3,)),
+        ],
+        ROUTE_LIMIT,
     )
     request, owners, ranks = route(list_length, list_owner.reshape(ROWS, SEGS), list_slot)
     asked = exchange(request)

time: 103 us -> 101 us (0.981)
  local copies, waits for them, and re-layouts: 3.53 us -> 1.47 us
    unnamed x12 -> x10, local copies, waits for them, and re-layouts: 3.53 us -> 1.47 us
where the time goes in v3:
time: 101 us
  Pallas kernels  50.7 us (50%)
  waiting for transfers between devices  16.1 us (16%)
  blocking collectives  16.1 us (16%)
  starting transfers between devices  15.8 us (16%)
  local copies, waits for them, and re-layouts  1.47 us (1%)
    all_to_all x1, blocking collectives, exchange(): lax.all_to_all(x.reshape(DEVS, 1, width), AXES, split_axis=0, concat_axis...  16.1 us
    pallas_call x1, Pallas kernels, body(): return (images, scatter(numbers, groups, incoming))  16.1 us
    all_to_all x2, waiting for transfers between devices, exchange(): lax.all_to_all(x.reshape(DEVS, 1, width), AXES, split_axis=0, concat_axis...  16.1 us
    all_to_all x2, starting transfers between devices, exchange(): lax.all_to_all(x.reshape(DEVS, 1, width), AXES, split_axis=0, concat_axis...  15.8 us
    pallas_call x1, Pallas kernels, body(): found, numbers, groups = gather(asked, packed)  13.8 us
    pallas_call x1, Pallas kernels, body(): images, outgoing = render(replies, hot, mark, keys, target)  13.3 us
    pallas_call x1, Pallas kernels, body(): pl.pallas_call(pack_kernel, name='pack', out_shape=shape((rows, 128), F32...  3.54 us
    pallas_call x1, Pallas kernels, body(): route(list_length, list_owner.reshape(ROWS, SEGS), list_slot)  3.45 us
  transfers between devices with their start and end apart: 2, of which 2 were waited for; matrix products, arithmetic and copies ran while one was open for 0% of the time, Pallas kernels for 4%

profile of v3, /device:TPU:1, one launch (start us, length us, event | category | flops | bytes accessed | tf_op | source)
XLA Modules:
  0.0 100.9 jit_solution(5152317037160783883)
XLA Ops:
  0.6 3.4 %route.1 = (s32[128,128]{1,0:T(8,128)}, f32[32,128]{1,0:T(8,128)}, f32[32,128]{1,0:T(8,128)}) custom-call(s32[4]{0:T(128)} %length_hbm.1, s32[32,128]{1,0:T(8,128)} %bitcast.15, s32[4,1024]{1,0:T(4,128)} %slot_hbm.1), custom_call_target="tpu_custom_call" | custom-call | tf_op jit(solution)/shard_map/route/pallas_call | solution.py:579
  4.1 11.5 %all-to-all-start = ((s32[128,1,128]{2,1,0:T(1,128)}), s32[128,1,128]{2,1,0:T(1,128)S(1)}, u32[]{:S(2)}, u32[]{:S(2)}) async-start(s32[128,1,128]{2,1,0:T(1,128)} %bitcast.14), calls=%async_computation | async-start | bytes 131072 | tf_op jit(solution)/shard_map/all_to_all | solution.py:563
  15.6 3.5 %pack.1.table_hbm = f32[8192,128]{1,0:T(8,128)} custom-call(f32[10,65536]{1,0:T(8,128)} %params_hbm.1), custom_call_target="tpu_custom_call" | custom-call | tf_op jit(solution)/shard_map/pack/pallas_call | solution.py:582
  19.1 0.0 copy-start.2
  19.2 0.0 copy-start.3
  19.2 0.0 copy-start.1
  19.2 6.0 %all-to-all-done = s32[128,1,128]{2,1,0:T(1,128)S(1)} async-done(((s32[128,1,128]{2,1,0:T(1,128)}), s32[128,1,128]{2,1,0:T(1,128)S(1)}, u32[]{:S(2)}, u32[]{:S(2)}) %all-to-all-start) | async-done | bytes 65568 | tf_op jit(solution)/shard_map/all_to_all | solution.py:563
  25.2 0.0 copy-start.4
  25.2 0.6 copy-done.4
  25.8 13.8 %gather.1 = (f32[640,128]{1,0:T(8,128)}, s32[128,128]{1,0:T(8,128)}, bf16[512,128]{1,0:T(8,128)(2,1)}) custom-call(s32[128,128]{1,0:T(8,128)} %bitcast.13, f32[8192,128]{1,0:T(8,128)} %pack.1.table_hbm), custom_call_target="tpu_custom_call" | custom-call | tf_op jit(solution)/shard_map/gather/pallas_call | solution.py:603
  39.6 4.3 %all-to-all-start.1 = ((f32[128,1,640]{2,1,0:T(1,128)}), f32[128,1,640]{2,1,0:T(1,128)S(1)}, u32[]{:S(2)}, u32[]{:S(2)}) async-start(f32[128,1,640]{2,1,0:T(1,128)} %bitcast.12), calls=%async_computation.1 | async-start | bytes 655360 | tf_op jit(solution)/shard_map/all_to_all | solution.py:563
  43.9 0.0 copy-done.2
  43.9 0.0 copy-done.3
  43.9 0.0 copy-start
  43.9 0.8 copy-done
  44.8 0.6 marks.1
  45.4 10.1 %all-to-all-done.1 = f32[128,1,640]{2,1,0:T(1,128)S(1)} async-done(((f32[128,1,640]{2,1,0:T(1,128)}), f32[128,1,640]{2,1,0:T(1,128)S(1)}, u32[]{:S(2)}, u32[]{:S(2)}) %all-to-all-start.1) | async-done | bytes 327712 | tf_op jit(solution)/shard_map/all_to_all | solution.py:563
  55.5 0.0 copy-done.1
  55.5 13.3 %render.1 = (f32[4,4,256]{2,1,0:T(4,128)}, f32[640,128]{1,0:T(8,128)S(1)}) custom-call(f32[640,128]{1,0:T(8,128)S(1)} %bitcast.9, bf16[256,4096]{1,0:T(8,128)(2,1)S(1)} %get-tuple-element.18.hot_ref, bf16[32,4096]{1,0:T(8,128)(2,1)S(1)} %get-tuple-element.19.mark_ref, f32[32,128]{1,0:T(8,128)S(1)} %get-tuple-element.20.key_ref, f32[4,4,256]{2,1,0:T(4,128)S(1)} %copy-done.1), custom_call_target="tpu_custom_call" | custom-call | tf_op jit(solution)/shard_map/render/pallas_call | solution.py:624
  68.7 16.1 %all_to_all.15 = f32[128,1,640]{2,1,0:T(1,128)} all-to-all(f32[128,1,640]{2,1,0:T(1,128)S(1)} %bitcast.10), channel_id=1, replica_groups=mesh['row'=4,'col'=32] {'row','col'}, dimensions={0} | all-to-all | bytes 655360 | tf_op jit(solution)/shard_map/all_to_all | solution.py:563
  84.8 16.1 %scatter.1 = f32[10,65536]{1,0:T(8,128)} custom-call(s32[128,128]{1,0:T(8,128)} %get-tuple-element.17.after_ref.row_number_ref, bf16[512,128]{1,0:T(8,128)(2,1)} %get-tuple-element.22.group_ref, f32[640,128]{1,0:T(8,128)} %bitcast.11), custom_call_target="tpu_custom_call" | custom-call | tf_op jit(solution)/shard_map/scatter/pallas_call | solution.py:637
Async XLA Ops:
  4.1 21.1 %all-to-all-start = ((s32[128,1,128]{2,1,0:T(1,128)}), s32[128,1,128]{2,1,0:T(1,128)S(1)}, u32[]{:S(2)}, u32[]{:S(2)}) async-start(s32[128,1,128]{2,1,0:T(1,128)} %bitcast.14), calls=%async_computation | async-start | bytes 131072 | tf_op jit(solution)/shard_map/all_to_all | solution.py:563
  19.1 24.8 %copy-start.2 = (f32[32,128]{1,0:T(8,128)S(1)}, f32[32,128]{1,0:T(8,128)}, u32[]{:S(2)}) copy-start(f32[32,128]{1,0:T(8,128)} %get-tuple-element.15.owner_ref) | copy-start | bytes 49156
  19.2 24.8 %copy-start.3 = (f32[32,128]{1,0:T(8,128)S(1)}, f32[32,128]{1,0:T(8,128)}, u32[]{:S(2)}) copy-start(f32[32,128]{1,0:T(8,128)} %get-tuple-element.16.rank_ref) | copy-start | bytes 49156
  19.2 36.3 %copy-start.1 = (f32[4,4,256]{2,1,0:T(4,128)S(1)}, f32[4,4,256]{2,1,0:T(4,128)}, u32[]{:S(2)}) copy-start(f32[4,4,256]{2,1,0:T(4,128)} %target_ref.1) | copy-start | bytes 49156
  25.2 0.6 copy-start.4
  39.6 15.9 %all-to-all-start.1 = ((f32[128,1,640]{2,1,0:T(1,128)}), f32[128,1,640]{2,1,0:T(1,128)S(1)}, u32[]{:S(2)}, u32[]{:S(2)}) async-start(f32[128,1,640]{2,1,0:T(1,128)} %bitcast.12), calls=%async_computation.1 | async-start | bytes 655360 | tf_op jit(solution)/shard_map/all_to_all | solution.py:563
  43.9 0.8 copy-start

commit v4 on v3

--- a/solution.py
+++ b/solution.py
@@ -15,7 +15,9 @@
 WIRE = 5
 GROUP = 16
 BLOCK = 16
-CHUNKS = ((0, 48), (48, 64))
+TIERS = ((0, 48), (48, RANKS))
+LOOK_UNROLL = 2
+ADD_UNROLL = 1
 STRETCH = 1024
 UNROLL = 4
 ROUTE_LIMIT = 63 << 20
@@ -212,18 +214,18 @@
     fill.wait()
 
     def source(src, carry):
+        mine_ref = row_ref.at[pl.ds(pl.multiple_of(src * RANKS, RANKS), RANKS)]
         count = number_ref[src, RANKS]
-        mine_ref = row_ref.at[pl.ds(pl.multiple_of(src * RANKS, RANKS), RANKS)]
-        for first, last in CHUNKS:
-
-            @pl.when(count > first)
+        for low, high in TIERS:
+
+            @pl.when((count > low) & (count <= high))
             def _():
-                for rank in range(first, last):
+                for rank in range(high):
                     mine_ref[rank : rank + 1, :] = table_ref[pl.ds(number_ref[src, rank], 1), :]
 
         return carry
 
-    lax.fori_loop(0, DEVS, source, 0)
+    lax.fori_loop(0, DEVS, source, 0, unroll=LOOK_UNROLL)
 
     def block(b, carry):
         base = pl.multiple_of(b * BLOCK * RANKS, BLOCK * RANKS)
@@ -293,15 +295,15 @@
     copy.wait()
 
     def source(src, carry):
+        mine_ref = row_ref.at[pl.ds(pl.multiple_of(src * RANKS, RANKS), RANKS)]
         count = number_ref[src, RANKS]
-        mine_ref = row_ref.at[pl.ds(pl.multiple_of(src * RANKS, RANKS), RANKS)]
-        for first, last in CHUNKS:
-
-            @pl.when(count > first)
+        for low, high in TIERS:
+
+            @pl.when((count > low) & (count <= high))
             def _():
-                for start in range(first, last, CHAINS):
+                for start in range(0, high, CHAINS):
                     news = []
-                    for i, ref in enumerate(totals[: last - start]):
+                    for i, ref in enumerate(totals[: high - start]):
                         row = number_ref[src, start + i]
                         news.append((row, mine_ref[start + i : start + i + 1, :] + ref[pl.ds(row, 1), :]))
                     for ref, (row, total) in zip(totals, news):
@@ -309,7 +311,7 @@
 
         return carry
 
-    lax.fori_loop(0, DEVS, source, 0)
+    lax.fori_loop(0, DEVS, source, 0, unroll=ADD_UNROLL)
 
     def close(i, carry):
         base = pl.multiple_of(i * STRETCH, STRETCH)
@@ -632,7 +634,7 @@
         scratch_shapes=staging
         + [pltpu.VMEM((DEVS // BLOCK, 128, 128), F32), pltpu.VMEM(splat_params.shape, F32), sems]
         + [table] * CHAINS,
-        compiler_params=pltpu.CompilerParams(vmem_limit_bytes=56 << 20),
+        compiler_params=pltpu.CompilerParams(vmem_limit_bytes=44 << 20),
     )
     return (images, scatter(numbers, groups, incoming))
 

time: 101 us -> 100 us (0.990)
  no operation moved by 1% of the time
where the time goes in v4:
time: 100 us; the launch traced here: 99.8 us
  Pallas kernels  49.7 us (50%)
  waiting for transfers between devices  16.2 us (16%)
  starting transfers between devices  15.9 us (16%)
  blocking collectives  15.9 us (16%)
  local copies, waits for them, and re-layouts  1.48 us (1%)
    all_to_all x2, waiting for transfers between devices, exchange(): lax.all_to_all(x.reshape(DEVS, 1, width), AXES, split_axis=0, concat_axis...  16.2 us
    all_to_all x2, starting transfers between devices, exchange(): lax.all_to_all(x.reshape(DEVS, 1, width), AXES, split_axis=0, concat_axis...  15.9 us
    all_to_all x1, blocking collectives, exchange(): lax.all_to_all(x.reshape(DEVS, 1, width), AXES, split_axis=0, concat_axis...  15.9 us
    pallas_call x1, Pallas kernels, body(): return (images, scatter(numbers, groups, incoming))  15.6 us
    pallas_call x1, Pallas kernels, body(): images, outgoing = render(replies, hot, mark, keys, target)  13.3 us
    pallas_call x1, Pallas kernels, body(): found, numbers, groups = gather(asked, packed)  13.2 us
    pallas_call x1, Pallas kernels, body(): pl.pallas_call(pack_kernel, name='pack', out_shape=shape((rows, 128), F32...  3.54 us
    pallas_call x1, Pallas kernels, body(): route(list_length, list_owner.reshape(ROWS, SEGS), list_slot)  3.44 us
  transfers between devices with their start and end apart: 2, of which 2 were waited for; matrix products, arithmetic and copies ran while one was open for 0% of the time, Pallas kernels for 4%

profile of v4, /device:TPU:1, one launch (start us, length us, event | category | flops | bytes accessed | tf_op | source)
XLA Modules:
  0.0 99.8 jit_solution(12626137571702781039)
XLA Ops:
  0.6 3.4 %route.1 = (s32[128,128]{1,0:T(8,128)}, f32[32,128]{1,0:T(8,128)}, f32[32,128]{1,0:T(8,128)}) custom-call(s32[4]{0:T(128)} %length_hbm.1, s32[32,128]{1,0:T(8,128)} %bitcast.15, s32[4,1024]{1,0:T(4,128)} %slot_hbm.1), custom_call_target="tpu_custom_call" | custom-call | tf_op jit(solution)/shard_map/route/pallas_call | solution.py:581
  4.1 11.5 %all-to-all-start = ((s32[128,1,128]{2,1,0:T(1,128)}), s32[128,1,128]{2,1,0:T(1,128)S(1)}, u32[]{:S(2)}, u32[]{:S(2)}) async-start(s32[128,1,128]{2,1,0:T(1,128)} %bitcast.14), calls=%async_computation | async-start | bytes 131072 | tf_op jit(solution)/shard_map/all_to_all | solution.py:565
  15.6 3.5 %pack.1.table_hbm = f32[8192,128]{1,0:T(8,128)} custom-call(f32[10,65536]{1,0:T(8,128)} %params_hbm.1), custom_call_target="tpu_custom_call" | custom-call | tf_op jit(solution)/shard_map/pack/pallas_call | solution.py:584
  19.1 0.0 copy-start.4
  19.1 0.0 copy-start.5
  19.2 0.0 copy-start.3
  19.2 6.0 %all-to-all-done = s32[128,1,128]{2,1,0:T(1,128)S(1)} async-done(((s32[128,1,128]{2,1,0:T(1,128)}), s32[128,1,128]{2,1,0:T(1,128)S(1)}, u32[]{:S(2)}, u32[]{:S(2)}) %all-to-all-start) | async-done | bytes 65568 | tf_op jit(solution)/shard_map/all_to_all | solution.py:565
  25.2 0.6 copy-done.6
  25.8 13.2 %gather.1 = (f32[640,128]{1,0:T(8,128)}, s32[128,128]{1,0:T(8,128)}, bf16[512,128]{1,0:T(8,128)(2,1)}) custom-call(s32[128,128]{1,0:T(8,128)} %bitcast.13, f32[8192,128]{1,0:T(8,128)} %pack.1.table_hbm), custom_call_target="tpu_custom_call" | custom-call | tf_op jit(solution)/shard_map/gather/pallas_call | solution.py:605
  39.0 0.0 copy-start.1
  39.0 0.0 copy-start.2
  39.0 4.4 %all-to-all-start.1 = ((f32[128,1,640]{2,1,0:T(1,128)}), f32[128,1,640]{2,1,0:T(1,128)S(1)}, u32[]{:S(2)}, u32[]{:S(2)}) async-start(f32[128,1,640]{2,1,0:T(1,128)} %bitcast.12), calls=%async_computation.1 | async-start | bytes 655360 | tf_op jit(solution)/shard_map/all_to_all | solution.py:565
  43.4 0.0 copy-done.4
  43.4 0.0 copy-done.5
  43.4 0.0 copy-start
  43.5 0.8 copy-done
  44.3 0.6 marks.1
  44.9 10.1 %all-to-all-done.1 = f32[128,1,640]{2,1,0:T(1,128)S(1)} async-done(((f32[128,1,640]{2,1,0:T(1,128)}), f32[128,1,640]{2,1,0:T(1,128)S(1)}, u32[]{:S(2)}, u32[]{:S(2)}) %all-to-all-start.1) | async-done | bytes 327712 | tf_op jit(solution)/shard_map/all_to_all | solution.py:565
  55.1 0.0 copy-done.3
  55.1 13.3 %render.1 = (f32[4,4,256]{2,1,0:T(4,128)}, f32[640,128]{1,0:T(8,128)S(1)}) custom-call(f32[640,128]{1,0:T(8,128)S(1)} %bitcast.10, bf16[256,4096]{1,0:T(8,128)(2,1)S(1)} %get-tuple-element.18.hot_ref, bf16[32,4096]{1,0:T(8,128)(2,1)S(1)} %get-tuple-element.19.mark_ref, f32[32,128]{1,0:T(8,128)S(1)} %get-tuple-element.20.key_ref, f32[4,4,256]{2,1,0:T(4,128)S(1)} %copy-done.3), custom_call_target="tpu_custom_call" | custom-call | tf_op jit(solution)/shard_map/render/pallas_call | solution.py:626
  68.3 15.9 %all_to_all.15 = f32[128,1,640]{2,1,0:T(1,128)S(1)} all-to-all(f32[128,1,640]{2,1,0:T(1,128)S(1)} %bitcast.11), channel_id=1, replica_groups=mesh['row'=4,'col'=32] {'row','col'}, dimensions={0} | all-to-all | bytes 655360 | tf_op jit(solution)/shard_map/all_to_all | solution.py:565
  84.2 0.0 copy-done.1
  84.2 0.0 copy-done.2
  84.2 15.6 %scatter.1 = f32[10,65536]{1,0:T(8,128)} custom-call(s32[128,128]{1,0:T(8,128)S(1)} %copy-done.1, bf16[512,128]{1,0:T(8,128)(2,1)S(1)} %copy-done.2, f32[640,128]{1,0:T(8,128)S(1)} %bitcast.9), custom_call_target="tpu_custom_call" | custom-call | tf_op jit(solution)/shard_map/scatter/pallas_call | solution.py:639
  (1 shorter events, 0.0 us)
Async XLA Ops:
  4.1 21.1 %all-to-all-start = ((s32[128,1,128]{2,1,0:T(1,128)}), s32[128,1,128]{2,1,0:T(1,128)S(1)}, u32[]{:S(2)}, u32[]{:S(2)}) async-start(s32[128,1,128]{2,1,0:T(1,128)} %bitcast.14), calls=%async_computation | async-start | bytes 131072 | tf_op jit(solution)/shard_map/all_to_all | solution.py:565
  19.1 24.3 %copy-start.4 = (f32[32,128]{1,0:T(8,128)S(1)}, f32[32,128]{1,0:T(8,128)}, u32[]{:S(2)}) copy-start(f32[32,128]{1,0:T(8,128)} %get-tuple-element.15.owner_ref) | copy-start | bytes 49156
  19.1 24.3 %copy-start.5 = (f32[32,128]{1,0:T(8,128)S(1)}, f32[32,128]{1,0:T(8,128)}, u32[]{:S(2)}) copy-start(f32[32,128]{1,0:T(8,128)} %get-tuple-element.16.rank_ref) | copy-start | bytes 49156
  19.2 35.9 %copy-start.3 = (f32[4,4,256]{2,1,0:T(4,128)S(1)}, f32[4,4,256]{2,1,0:T(4,128)}, u32[]{:S(2)}) copy-start(f32[4,4,256]{2,1,0:T(4,128)} %target_ref.1) | copy-start | bytes 49156
  25.2 0.6 copy-start.6
  39.0 45.2 %copy-start.1 = (s32[128,128]{1,0:T(8,128)S(1)}, s32[128,128]{1,0:T(8,128)}, u32[]{:S(2)}) copy-start(s32[128,128]{1,0:T(8,128)} %get-tuple-element.17.after_ref.row_number_ref) | copy-start | bytes 196612
  39.0 45.2 %copy-start.2 = (bf16[512,128]{1,0:T(8,128)(2,1)S(1)}, bf16[512,128]{1,0:T(8,128)(2,1)}, u32[]{:S(2)}) copy-start(bf16[512,128]{1,0:T(8,128)(2,1)} %get-tuple-element.22.group_ref) | copy-start | bytes 393220
  39.0 16.0 %all-to-all-start.1 = ((f32[128,1,640]{2,1,0:T(1,128)}), f32[128,1,640]{2,1,0:T(1,128)S(1)}, u32[]{:S(2)}, u32[]{:S(2)}) async-start(f32[128,1,640]{2,1,0:T(1,128)} %bitcast.12), calls=%async_computation.1 | async-start | bytes 655360 | tf_op jit(solution)/shard_map/all_to_all | solution.py:565
  43.4 0.8 copy-start

commit v5 on v4

--- a/solution.py
+++ b/solution.py
@@ -601,7 +601,7 @@
     sems = pltpu.SemaphoreType.DMA((2,))
     numbers = shape((DEVS, 128), jnp.int32)
     groups = shape((DEVS // BLOCK * RANKS, DEVS), BF16)
-    gather = call(gather_kernel, "gather", [vmem(), hbm()], (wire, numbers, groups), staging + [table, sems], 60 << 20)
+    gather = call(gather_kernel, "gather", [vmem(), hbm()], (wire, numbers, groups), staging + [table, sems], 51 << 20)
     found, numbers, groups = gather(asked, packed)
     replies = exchange(found)
     entries = ROWS * SEGS

time: 100 us -> 98.3 us (0.983)
  Pallas kernels: 49.7 us -> 48.2 us
  local copies, waits for them, and re-layouts: 1.48 us -> 0.02 us
    unnamed x14 -> x6, local copies, waits for them, and re-layouts: 1.48 us -> 0.02 us
where the time goes in v5:
time: 98.3 us; the launch traced here: 97.9 us
  Pallas kernels  48.2 us (49%)
  waiting for transfers between devices  17.1 us (17%)
  starting transfers between devices  16 us (16%)
  blocking collectives  15.9 us (16%)
    all_to_all x2, waiting for transfers between devices, exchange(): lax.all_to_all(x.reshape(DEVS, 1, width), AXES, split_axis=0, concat_axis...  17.1 us
    all_to_all x2, starting transfers between devices, exchange(): lax.all_to_all(x.reshape(DEVS, 1, width), AXES, split_axis=0, concat_axis...  16 us
    all_to_all x1, blocking collectives, exchange(): lax.all_to_all(x.reshape(DEVS, 1, width), AXES, split_axis=0, concat_axis...  15.9 us
    pallas_call x1, Pallas kernels, body(): return (images, scatter(numbers, groups, incoming))  15 us
    pallas_call x1, Pallas kernels, body(): images, outgoing = render(replies, hot, mark, keys, target)  13.3 us
    pallas_call x1, Pallas kernels, body(): found, numbers, groups = gather(asked, packed)  12.4 us
    pallas_call x1, Pallas kernels, body(): pl.pallas_call(pack_kernel, name='pack', out_shape=shape((rows, 128), F32...  3.54 us
    pallas_call x1, Pallas kernels, body(): route(list_length, list_owner.reshape(ROWS, SEGS), list_slot)  3.44 us
  transfers between devices with their start and end apart: 2, of which 2 were waited for; matrix products, arithmetic and copies ran while one was open for 0% of the time, Pallas kernels for 4%

profile of v5, /device:TPU:1, one launch (start us, length us, event | category | flops | bytes accessed | tf_op | source)
XLA Modules:
  0.0 97.9 jit_solution(11609808369127072260)
XLA Ops:
  0.6 3.4 %route.1 = (s32[128,128]{1,0:T(8,128)}, f32[32,128]{1,0:T(8,128)}, f32[32,128]{1,0:T(8,128)}) custom-call(s32[4]{0:T(128)} %length_hbm.1, s32[32,128]{1,0:T(8,128)} %bitcast.14, s32[4,1024]{1,0:T(4,128)} %slot_hbm.1), custom_call_target="tpu_custom_call" | custom-call | tf_op jit(solution)/shard_map/route/pallas_call | solution.py:581
  4.1 11.5 %all-to-all-start = ((s32[128,1,128]{2,1,0:T(1,128)}), s32[128,1,128]{2,1,0:T(1,128)S(1)}, u32[]{:S(2)}, u32[]{:S(2)}) async-start(s32[128,1,128]{2,1,0:T(1,128)} %bitcast.13), calls=%async_computation | async-start | bytes 131072 | tf_op jit(solution)/shard_map/all_to_all | solution.py:565
  15.6 3.5 %pack.1.table_hbm = f32[8192,128]{1,0:T(8,128)} custom-call(f32[10,65536]{1,0:T(8,128)} %params_hbm.1), custom_call_target="tpu_custom_call" | custom-call | tf_op jit(solution)/shard_map/pack/pallas_call | solution.py:584
  19.1 0.0 copy-start.1
  19.2 0.0 copy-start.2
  19.2 0.0 copy-start
  19.2 6.0 %all-to-all-done = s32[128,1,128]{2,1,0:T(1,128)S(1)} async-done(((s32[128,1,128]{2,1,0:T(1,128)}), s32[128,1,128]{2,1,0:T(1,128)S(1)}, u32[]{:S(2)}, u32[]{:S(2)}) %all-to-all-start) | async-done | bytes 65568 | tf_op jit(solution)/shard_map/all_to_all | solution.py:565
  25.2 12.4 %gather.1 = (f32[640,128]{1,0:T(8,128)}, s32[128,128]{1,0:T(8,128)S(1)}, bf16[512,128]{1,0:T(8,128)(2,1)S(1)}) custom-call(s32[128,128]{1,0:T(8,128)S(1)} %bitcast.12, f32[8192,128]{1,0:T(8,128)} %pack.1.table_hbm), custom_call_target="tpu_custom_call" | custom-call | tf_op jit(solution)/shard_map/gather/pallas_call | solution.py:605
  37.6 4.5 %all-to-all-start.1 = ((f32[128,1,640]{2,1,0:T(1,128)}), f32[128,1,640]{2,1,0:T(1,128)S(1)}, u32[]{:S(2)}, u32[]{:S(2)}) async-start(f32[128,1,640]{2,1,0:T(1,128)} %bitcast.4), calls=%async_computation.1 | async-start | bytes 655360 | tf_op jit(solution)/shard_map/all_to_all | solution.py:565
  42.1 0.0 copy-done.1
  42.1 0.0 copy-done.2
  42.1 0.6 marks.1
  42.7 11.0 %all-to-all-done.1 = f32[128,1,640]{2,1,0:T(1,128)S(1)} async-done(((f32[128,1,640]{2,1,0:T(1,128)}), f32[128,1,640]{2,1,0:T(1,128)S(1)}, u32[]{:S(2)}, u32[]{:S(2)}) %all-to-all-start.1) | async-done | bytes 327712 | tf_op jit(solution)/shard_map/all_to_all | solution.py:565
  53.8 0.0 copy-done
  53.8 13.3 %render.1 = (f32[4,4,256]{2,1,0:T(4,128)}, f32[640,128]{1,0:T(8,128)S(1)}) custom-call(f32[640,128]{1,0:T(8,128)S(1)} %bitcast.10, bf16[256,4096]{1,0:T(8,128)(2,1)S(1)} %get-tuple-element.18.hot_ref, bf16[32,4096]{1,0:T(8,128)(2,1)S(1)} %get-tuple-element.19.mark_ref, f32[32,128]{1,0:T(8,128)S(1)} %get-tuple-element.20.key_ref, f32[4,4,256]{2,1,0:T(4,128)S(1)} %copy-done), custom_call_target="tpu_custom_call" | custom-call | tf_op jit(solution)/shard_map/render/pallas_call | solution.py:626
  67.0 15.9 %all_to_all.15 = f32[128,1,640]{2,1,0:T(1,128)S(1)} all-to-all(f32[128,1,640]{2,1,0:T(1,128)S(1)} %bitcast.11), channel_id=1, replica_groups=mesh['row'=4,'col'=32] {'row','col'}, dimensions={0} | all-to-all | bytes 655360 | tf_op jit(solution)/shard_map/all_to_all | solution.py:565
  82.9 15.0 %scatter.1 = f32[10,65536]{1,0:T(8,128)} custom-call(s32[128,128]{1,0:T(8,128)S(1)} %get-tuple-element.17.after_ref.row_number_ref, bf16[512,128]{1,0:T(8,128)(2,1)S(1)} %get-tuple-element.22.group_ref, f32[640,128]{1,0:T(8,128)S(1)} %bitcast.9), custom_call_target="tpu_custom_call" | custom-call | tf_op jit(solution)/shard_map/scatter/pallas_call | solution.py:639
Async XLA Ops:
  4.1 21.1 %all-to-all-start = ((s32[128,1,128]{2,1,0:T(1,128)}), s32[128,1,128]{2,1,0:T(1,128)S(1)}, u32[]{:S(2)}, u32[]{:S(2)}) async-start(s32[128,1,128]{2,1,0:T(1,128)} %bitcast.13), calls=%async_computation | async-start | bytes 131072 | tf_op jit(solution)/shard_map/all_to_all | solution.py:565
  19.1 22.9 %copy-start.1 = (f32[32,128]{1,0:T(8,128)S(1)}, f32[32,128]{1,0:T(8,128)}, u32[]{:S(2)}) copy-start(f32[32,128]{1,0:T(8,128)} %get-tuple-element.15.owner_ref) | copy-start | bytes 49156
  19.2 22.9 %copy-start.2 = (f32[32,128]{1,0:T(8,128)S(1)}, f32[32,128]{1,0:T(8,128)}, u32[]{:S(2)}) copy-start(f32[32,128]{1,0:T(8,128)} %get-tuple-element.16.rank_ref) | copy-start | bytes 49156
  19.2 34.6 %copy-start = (f32[4,4,256]{2,1,0:T(4,128)S(1)}, f32[4,4,256]{2,1,0:T(4,128)}, u32[]{:S(2)}) copy-start(f32[4,4,256]{2,1,0:T(4,128)} %target_ref.1) | copy-start | bytes 49156
  37.6 16.2 %all-to-all-start.1 = ((f32[128,1,640]{2,1,0:T(1,128)}), f32[128,1,640]{2,1,0:T(1,128)S(1)}, u32[]{:S(2)}, u32[]{:S(2)}) async-start(f32[128,1,640]{2,1,0:T(1,128)} %bitcast.4), calls=%async_computation.1 | async-start | bytes 655360 | tf_op jit(solution)/shard_map/all_to_all | solution.py:565

commit v6 on v5

--- a/solution.py
+++ b/solution.py
@@ -16,8 +16,8 @@
 GROUP = 16
 BLOCK = 16
 TIERS = ((0, 48), (48, RANKS))
-LOOK_UNROLL = 2
-ADD_UNROLL = 1
+LOOK_UNROLL = 8
+ADD_UNROLL = 4
 STRETCH = 1024
 UNROLL = 4
 ROUTE_LIMIT = 63 << 20

time: 98.3 us -> 97.9 us (level)
  no operation moved by 1% of the time
where the time goes in v6:
time: 97.9 us; the launch traced here: 97.5 us
  Pallas kernels  48 us (49%)
  waiting for transfers between devices  16.9 us (17%)
  starting transfers between devices  15.9 us (16%)
  blocking collectives  15.9 us (16%)
    all_to_all x2, waiting for transfers between devices, exchange(): lax.all_to_all(x.reshape(DEVS, 1, width), AXES, split_axis=0, concat_axis...  16.9 us
    all_to_all x2, starting transfers between devices, exchange(): lax.all_to_all(x.reshape(DEVS, 1, width), AXES, split_axis=0, concat_axis...  15.9 us
    all_to_all x1, blocking collectives, exchange(): lax.all_to_all(x.reshape(DEVS, 1, width), AXES, split_axis=0, concat_axis...  15.9 us
    pallas_call x1, Pallas kernels, body(): return (images, scatter(numbers, groups, incoming))  15.1 us
    pallas_call x1, Pallas kernels, body(): images, outgoing = render(replies, hot, mark, keys, target)  13.3 us
    pallas_call x1, Pallas kernels, body(): found, numbers, groups = gather(asked, packed)  12.1 us
    pallas_call x1, Pallas kernels, body(): pl.pallas_call(pack_kernel, name='pack', out_shape=shape((rows, 128), F32...  3.54 us
    pallas_call x1, Pallas kernels, body(): route(list_length, list_owner.reshape(ROWS, SEGS), list_slot)  3.44 us
  transfers between devices with their start and end apart: 2, of which 2 were waited for; matrix products, arithmetic and copies ran while one was open for 0% of the time, Pallas kernels for 4%

profile of v6, /device:TPU:1, one launch (start us, length us, event | category | flops | bytes accessed | tf_op | source)
XLA Modules:
  0.0 97.5 jit_solution(10833285884589358469)
XLA Ops:
  0.6 3.4 %route.1 = (s32[128,128]{1,0:T(8,128)}, f32[32,128]{1,0:T(8,128)}, f32[32,128]{1,0:T(8,128)}) custom-call(s32[4]{0:T(128)} %length_hbm.1, s32[32,128]{1,0:T(8,128)} %bitcast.14, s32[4,1024]{1,0:T(4,128)} %slot_hbm.1), custom_call_target="tpu_custom_call" | custom-call | tf_op jit(solution)/shard_map/route/pallas_call | solution.py:581
  4.1 11.5 %all-to-all-start = ((s32[128,1,128]{2,1,0:T(1,128)}), s32[128,1,128]{2,1,0:T(1,128)S(1)}, u32[]{:S(2)}, u32[]{:S(2)}) async-start(s32[128,1,128]{2,1,0:T(1,128)} %bitcast.13), calls=%async_computation | async-start | bytes 131072 | tf_op jit(solution)/shard_map/all_to_all | solution.py:565
  15.6 3.5 %pack.1.table_hbm = f32[8192,128]{1,0:T(8,128)} custom-call(f32[10,65536]{1,0:T(8,128)} %params_hbm.1), custom_call_target="tpu_custom_call" | custom-call | tf_op jit(solution)/shard_map/pack/pallas_call | solution.py:584
  19.1 0.0 copy-start.1
  19.2 0.0 copy-start.2
  19.2 0.0 copy-start
  19.2 6.0 %all-to-all-done = s32[128,1,128]{2,1,0:T(1,128)S(1)} async-done(((s32[128,1,128]{2,1,0:T(1,128)}), s32[128,1,128]{2,1,0:T(1,128)S(1)}, u32[]{:S(2)}, u32[]{:S(2)}) %all-to-all-start) | async-done | bytes 65568 | tf_op jit(solution)/shard_map/all_to_all | solution.py:565
  25.2 12.1 %gather.1 = (f32[640,128]{1,0:T(8,128)}, s32[128,128]{1,0:T(8,128)S(1)}, bf16[512,128]{1,0:T(8,128)(2,1)S(1)}) custom-call(s32[128,128]{1,0:T(8,128)S(1)} %bitcast.12, f32[8192,128]{1,0:T(8,128)} %pack.1.table_hbm), custom_call_target="tpu_custom_call" | custom-call | tf_op jit(solution)/shard_map/gather/pallas_call | solution.py:605
  37.3 4.4 %all-to-all-start.1 = ((f32[128,1,640]{2,1,0:T(1,128)}), f32[128,1,640]{2,1,0:T(1,128)S(1)}, u32[]{:S(2)}, u32[]{:S(2)}) async-start(f32[128,1,640]{2,1,0:T(1,128)} %bitcast.4), calls=%async_computation.1 | async-start | bytes 655360 | tf_op jit(solution)/shard_map/all_to_all | solution.py:565
  41.7 0.0 copy-done.1
  41.7 0.0 copy-done.2
  41.7 0.6 marks.1
  42.3 10.9 %all-to-all-done.1 = f32[128,1,640]{2,1,0:T(1,128)S(1)} async-done(((f32[128,1,640]{2,1,0:T(1,128)}), f32[128,1,640]{2,1,0:T(1,128)S(1)}, u32[]{:S(2)}, u32[]{:S(2)}) %all-to-all-start.1) | async-done | bytes 327712 | tf_op jit(solution)/shard_map/all_to_all | solution.py:565
  53.2 0.0 copy-done
  53.2 13.3 %render.1 = (f32[4,4,256]{2,1,0:T(4,128)}, f32[640,128]{1,0:T(8,128)S(1)}) custom-call(f32[640,128]{1,0:T(8,128)S(1)} %bitcast.10, bf16[256,4096]{1,0:T(8,128)(2,1)S(1)} %get-tuple-element.18.hot_ref, bf16[32,4096]{1,0:T(8,128)(2,1)S(1)} %get-tuple-element.19.mark_ref, f32[32,128]{1,0:T(8,128)S(1)} %get-tuple-element.20.key_ref, f32[4,4,256]{2,1,0:T(4,128)S(1)} %copy-done), custom_call_target="tpu_custom_call" | custom-call | tf_op jit(solution)/shard_map/render/pallas_call | solution.py:626
  66.5 15.9 %all_to_all.15 = f32[128,1,640]{2,1,0:T(1,128)S(1)} all-to-all(f32[128,1,640]{2,1,0:T(1,128)S(1)} %bitcast.11), channel_id=1, replica_groups=mesh['row'=4,'col'=32] {'row','col'}, dimensions={0} | all-to-all | bytes 655360 | tf_op jit(solution)/shard_map/all_to_all | solution.py:565
  82.4 15.1 %scatter.1 = f32[10,65536]{1,0:T(8,128)} custom-call(s32[128,128]{1,0:T(8,128)S(1)} %get-tuple-element.17.after_ref.row_number_ref, bf16[512,128]{1,0:T(8,128)(2,1)S(1)} %get-tuple-element.22.group_ref, f32[640,128]{1,0:T(8,128)S(1)} %bitcast.9), custom_call_target="tpu_custom_call" | custom-call | tf_op jit(solution)/shard_map/scatter/pallas_call | solution.py:639
Async XLA Ops:
  4.1 21.1 %all-to-all-start = ((s32[128,1,128]{2,1,0:T(1,128)}), s32[128,1,128]{2,1,0:T(1,128)S(1)}, u32[]{:S(2)}, u32[]{:S(2)}) async-start(s32[128,1,128]{2,1,0:T(1,128)} %bitcast.13), calls=%async_computation | async-start | bytes 131072 | tf_op jit(solution)/shard_map/all_to_all | solution.py:565
  19.1 22.5 %copy-start.1 = (f32[32,128]{1,0:T(8,128)S(1)}, f32[32,128]{1,0:T(8,128)}, u32[]{:S(2)}) copy-start(f32[32,128]{1,0:T(8,128)} %get-tuple-element.15.owner_ref) | copy-start | bytes 49156
  19.2 22.5 %copy-start.2 = (f32[32,128]{1,0:T(8,128)S(1)}, f32[32,128]{1,0:T(8,128)}, u32[]{:S(2)}) copy-start(f32[32,128]{1,0:T(8,128)} %get-tuple-element.16.rank_ref) | copy-start | bytes 49156
  19.2 34.1 %copy-start = (f32[4,4,256]{2,1,0:T(4,128)S(1)}, f32[4,4,256]{2,1,0:T(4,128)}, u32[]{:S(2)}) copy-start(f32[4,4,256]{2,1,0:T(4,128)} %target_ref.1) | copy-start | bytes 49156
  37.3 15.9 %all-to-all-start.1 = ((f32[128,1,640]{2,1,0:T(1,128)}), f32[128,1,640]{2,1,0:T(1,128)S(1)}, u32[]{:S(2)}, u32[]{:S(2)}) async-start(f32[128,1,640]{2,1,0:T(1,128)} %bitcast.4), calls=%async_computation.1 | async-start | bytes 655360 | tf_op jit(solution)/shard_map/all_to_all | solution.py:565

commit v7 on v6

--- a/solution.py
+++ b/solution.py
@@ -26,7 +26,7 @@
 FETCH = 4096
 SPREAD = 4096
 BACK = 8
-CHAINS = 6
+CHAINS = 8
 LOG2E = 1.4426950408889634
 F32 = jnp.float32
 BF16 = jnp.bfloat16
@@ -634,7 +634,7 @@
         scratch_shapes=staging
         + [pltpu.VMEM((DEVS // BLOCK, 128, 128), F32), pltpu.VMEM(splat_params.shape, F32), sems]
         + [table] * CHAINS,
-        compiler_params=pltpu.CompilerParams(vmem_limit_bytes=44 << 20),
+        compiler_params=pltpu.CompilerParams(vmem_limit_bytes=49 << 20),
     )
     return (images, scatter(numbers, groups, incoming))
 

time: 97.9 us -> 98 us (level)
  no operation moved by 1% of the time
where the time goes in v7:
time: 98 us; the launch traced here: 97.5 us
  Pallas kernels  48.4 us (49%)
  waiting for transfers between devices  16.9 us (17%)
  blocking collectives  15.9 us (16%)
  starting transfers between devices  15.5 us (16%)
    all_to_all x2, waiting for transfers between devices, exchange(): lax.all_to_all(x.reshape(DEVS, 1, width), AXES, split_axis=0, concat_axis...  16.9 us
    all_to_all x1, blocking collectives, exchange(): lax.all_to_all(x.reshape(DEVS, 1, width), AXES, split_axis=0, concat_axis...  15.9 us
    all_to_all x2, starting transfers between devices, exchange(): lax.all_to_all(x.reshape(DEVS, 1, width), AXES, split_axis=0, concat_axis...  15.5 us
    pallas_call x1, Pallas kernels, body(): return (images, scatter(numbers, groups, incoming))  15.1 us
    pallas_call x1, Pallas kernels, body(): images, outgoing = render(replies, hot, mark, keys, target)  13.3 us
    pallas_call x1, Pallas kernels, body(): found, numbers, groups = gather(asked, packed)  12.4 us
    pallas_call x1, Pallas kernels, body(): pl.pallas_call(pack_kernel, name='pack', out_shape=shape((rows, 128), F32...  3.54 us
    pallas_call x1, Pallas kernels, body(): route(list_length, list_owner.reshape(ROWS, SEGS), list_slot)  3.44 us
  transfers between devices with their start and end apart: 2, of which 2 were waited for; matrix products, arithmetic and copies ran while one was open for 0% of the time, Pallas kernels for 4%

profile of v7, /device:TPU:1, one launch (start us, length us, event | category | flops | bytes accessed | tf_op | source)
XLA Modules:
  0.0 97.5 jit_solution(751805593523674943)
XLA Ops:
  0.6 3.4 %route.1 = (s32[128,128]{1,0:T(8,128)}, f32[32,128]{1,0:T(8,128)}, f32[32,128]{1,0:T(8,128)}) custom-call(s32[4]{0:T(128)} %length_hbm.1, s32[32,128]{1,0:T(8,128)} %bitcast.14, s32[4,1024]{1,0:T(4,128)} %slot_hbm.1), custom_call_target="tpu_custom_call" | custom-call | tf_op jit(solution)/shard_map/route/pallas_call | solution.py:581
  4.1 11.5 %all-to-all-start = ((s32[128,1,128]{2,1,0:T(1,128)}), s32[128,1,128]{2,1,0:T(1,128)S(1)}, u32[]{:S(2)}, u32[]{:S(2)}) async-start(s32[128,1,128]{2,1,0:T(1,128)} %bitcast.13), calls=%async_computation | async-start | bytes 131072 | tf_op jit(solution)/shard_map/all_to_all | solution.py:565
  15.6 3.5 %pack.1.table_hbm = f32[8192,128]{1,0:T(8,128)} custom-call(f32[10,65536]{1,0:T(8,128)} %params_hbm.1), custom_call_target="tpu_custom_call" | custom-call | tf_op jit(solution)/shard_map/pack/pallas_call | solution.py:584
  19.1 0.0 copy-start.1
  19.2 0.0 copy-start.2
  19.2 0.0 copy-start
  19.2 6.0 %all-to-all-done = s32[128,1,128]{2,1,0:T(1,128)S(1)} async-done(((s32[128,1,128]{2,1,0:T(1,128)}), s32[128,1,128]{2,1,0:T(1,128)S(1)}, u32[]{:S(2)}, u32[]{:S(2)}) %all-to-all-start) | async-done | bytes 65568 | tf_op jit(solution)/shard_map/all_to_all | solution.py:565
  25.2 12.4 %gather.1 = (f32[640,128]{1,0:T(8,128)}, s32[128,128]{1,0:T(8,128)S(1)}, bf16[512,128]{1,0:T(8,128)(2,1)S(1)}) custom-call(s32[128,128]{1,0:T(8,128)S(1)} %bitcast.12, f32[8192,128]{1,0:T(8,128)} %pack.1.table_hbm), custom_call_target="tpu_custom_call" | custom-call | tf_op jit(solution)/shard_map/gather/pallas_call | solution.py:605
  37.6 4.0 %all-to-all-start.1 = ((f32[128,1,640]{2,1,0:T(1,128)}), f32[128,1,640]{2,1,0:T(1,128)S(1)}, u32[]{:S(2)}, u32[]{:S(2)}) async-start(f32[128,1,640]{2,1,0:T(1,128)} %bitcast.4), calls=%async_computation.1 | async-start | bytes 655360 | tf_op jit(solution)/shard_map/all_to_all | solution.py:565
  41.7 0.0 copy-done.1
  41.7 0.0 copy-done.2
  41.7 0.6 marks.1
  42.4 10.9 %all-to-all-done.1 = f32[128,1,640]{2,1,0:T(1,128)S(1)} async-done(((f32[128,1,640]{2,1,0:T(1,128)}), f32[128,1,640]{2,1,0:T(1,128)S(1)}, u32[]{:S(2)}, u32[]{:S(2)}) %all-to-all-start.1) | async-done | bytes 327712 | tf_op jit(solution)/shard_map/all_to_all | solution.py:565
  53.3 0.0 copy-done
  53.3 13.3 %render.1 = (f32[4,4,256]{2,1,0:T(4,128)}, f32[640,128]{1,0:T(8,128)S(1)}) custom-call(f32[640,128]{1,0:T(8,128)S(1)} %bitcast.10, bf16[256,4096]{1,0:T(8,128)(2,1)S(1)} %get-tuple-element.18.hot_ref, bf16[32,4096]{1,0:T(8,128)(2,1)S(1)} %get-tuple-element.19.mark_ref, f32[32,128]{1,0:T(8,128)S(1)} %get-tuple-element.20.key_ref, f32[4,4,256]{2,1,0:T(4,128)S(1)} %copy-done), custom_call_target="tpu_custom_call" | custom-call | tf_op jit(solution)/shard_map/render/pallas_call | solution.py:626
  66.5 15.9 %all_to_all.15 = f32[128,1,640]{2,1,0:T(1,128)S(1)} all-to-all(f32[128,1,640]{2,1,0:T(1,128)S(1)} %bitcast.11), channel_id=1, replica_groups=mesh['row'=4,'col'=32] {'row','col'}, dimensions={0} | all-to-all | bytes 655360 | tf_op jit(solution)/shard_map/all_to_all | solution.py:565
  82.4 15.1 %scatter.1 = f32[10,65536]{1,0:T(8,128)} custom-call(s32[128,128]{1,0:T(8,128)S(1)} %get-tuple-element.17.after_ref.row_number_ref, bf16[512,128]{1,0:T(8,128)(2,1)S(1)} %get-tuple-element.22.group_ref, f32[640,128]{1,0:T(8,128)S(1)} %bitcast.9), custom_call_target="tpu_custom_call" | custom-call | tf_op jit(solution)/shard_map/scatter/pallas_call | solution.py:639
Async XLA Ops:
  4.1 21.1 %all-to-all-start = ((s32[128,1,128]{2,1,0:T(1,128)}), s32[128,1,128]{2,1,0:T(1,128)S(1)}, u32[]{:S(2)}, u32[]{:S(2)}) async-start(s32[128,1,128]{2,1,0:T(1,128)} %bitcast.13), calls=%async_computation | async-start | bytes 131072 | tf_op jit(solution)/shard_map/all_to_all | solution.py:565
  19.1 22.6 %copy-start.1 = (f32[32,128]{1,0:T(8,128)S(1)}, f32[32,128]{1,0:T(8,128)}, u32[]{:S(2)}) copy-start(f32[32,128]{1,0:T(8,128)} %get-tuple-element.15.owner_ref) | copy-start | bytes 49156
  19.2 22.5 %copy-start.2 = (f32[32,128]{1,0:T(8,128)S(1)}, f32[32,128]{1,0:T(8,128)}, u32[]{:S(2)}) copy-start(f32[32,128]{1,0:T(8,128)} %get-tuple-element.16.rank_ref) | copy-start | bytes 49156
  19.2 34.1 %copy-start = (f32[4,4,256]{2,1,0:T(4,128)S(1)}, f32[4,4,256]{2,1,0:T(4,128)}, u32[]{:S(2)}) copy-start(f32[4,4,256]{2,1,0:T(4,128)} %target_ref.1) | copy-start | bytes 49156
  37.6 15.6 %all-to-all-start.1 = ((f32[128,1,640]{2,1,0:T(1,128)}), f32[128,1,640]{2,1,0:T(1,128)S(1)}, u32[]{:S(2)}, u32[]{:S(2)}) async-start(f32[128,1,640]{2,1,0:T(1,128)} %bitcast.4), calls=%async_computation.1 | async-start | bytes 655360 | tf_op jit(solution)/shard_map/all_to_all | solution.py:565

commit v8 on v7

--- a/solution.py
+++ b/solution.py
@@ -16,8 +16,8 @@
 GROUP = 16
 BLOCK = 16
 TIERS = ((0, 48), (48, RANKS))
-LOOK_UNROLL = 8
-ADD_UNROLL = 4
+LOOK_UNROLL = 16
+ADD_UNROLL = 8
 STRETCH = 1024
 UNROLL = 4
 ROUTE_LIMIT = 63 << 20

time: 98 us -> 97.8 us (level)
  no operation moved by 1% of the time
where the time goes in v8:
time: 97.8 us; the launch traced here: 97.5 us
  Pallas kernels  48.3 us (49%)
  waiting for transfers between devices  16.9 us (17%)
  blocking collectives  15.9 us (16%)
  starting transfers between devices  15.5 us (16%)
    all_to_all x2, waiting for transfers between devices, exchange(): lax.all_to_all(x.reshape(DEVS, 1, width), AXES, split_axis=0, concat_axis...  16.9 us
    all_to_all x1, blocking collectives, exchange(): lax.all_to_all(x.reshape(DEVS, 1, width), AXES, split_axis=0, concat_axis...  15.9 us
    all_to_all x2, starting transfers between devices, exchange(): lax.all_to_all(x.reshape(DEVS, 1, width), AXES, split_axis=0, concat_axis...  15.5 us
    pallas_call x1, Pallas kernels, body(): return (images, scatter(numbers, groups, incoming))  15 us
    pallas_call x1, Pallas kernels, body(): images, outgoing = render(replies, hot, mark, keys, target)  13.3 us
    pallas_call x1, Pallas kernels, body(): found, numbers, groups = gather(asked, packed)  12.4 us
    pallas_call x1, Pallas kernels, body(): pl.pallas_call(pack_kernel, name='pack', out_shape=shape((rows, 128), F32...  3.54 us
    pallas_call x1, Pallas kernels, body(): route(list_length, list_owner.reshape(ROWS, SEGS), list_slot)  3.44 us
  transfers between devices with their start and end apart: 2, of which 2 were waited for; matrix products, arithmetic and copies ran while one was open for 0% of the time, Pallas kernels for 4%

profile of v8, /device:TPU:1, one launch (start us, length us, event | category | flops | bytes accessed | tf_op | source)
XLA Modules:
  0.0 97.5 jit_solution(6085776557406130842)
XLA Ops:
  0.6 3.4 %route.1 = (s32[128,128]{1,0:T(8,128)}, f32[32,128]{1,0:T(8,128)}, f32[32,128]{1,0:T(8,128)}) custom-call(s32[4]{0:T(128)} %length_hbm.1, s32[32,128]{1,0:T(8,128)} %bitcast.14, s32[4,1024]{1,0:T(4,128)} %slot_hbm.1), custom_call_target="tpu_custom_call" | custom-call | tf_op jit(solution)/shard_map/route/pallas_call | solution.py:581
  4.1 11.5 %all-to-all-start = ((s32[128,1,128]{2,1,0:T(1,128)}), s32[128,1,128]{2,1,0:T(1,128)S(1)}, u32[]{:S(2)}, u32[]{:S(2)}) async-start(s32[128,1,128]{2,1,0:T(1,128)} %bitcast.13), calls=%async_computation | async-start | bytes 131072 | tf_op jit(solution)/shard_map/all_to_all | solution.py:565
  15.6 3.5 %pack.1.table_hbm = f32[8192,128]{1,0:T(8,128)} custom-call(f32[10,65536]{1,0:T(8,128)} %params_hbm.1), custom_call_target="tpu_custom_call" | custom-call | tf_op jit(solution)/shard_map/pack/pallas_call | solution.py:584
  19.1 0.0 copy-start.1
  19.2 0.0 copy-start.2
  19.2 0.0 copy-start
  19.2 6.0 %all-to-all-done = s32[128,1,128]{2,1,0:T(1,128)S(1)} async-done(((s32[128,1,128]{2,1,0:T(1,128)}), s32[128,1,128]{2,1,0:T(1,128)S(1)}, u32[]{:S(2)}, u32[]{:S(2)}) %all-to-all-start) | async-done | bytes 65568 | tf_op jit(solution)/shard_map/all_to_all | solution.py:565
  25.2 12.4 %gather.1 = (f32[640,128]{1,0:T(8,128)}, s32[128,128]{1,0:T(8,128)S(1)}, bf16[512,128]{1,0:T(8,128)(2,1)S(1)}) custom-call(s32[128,128]{1,0:T(8,128)S(1)} %bitcast.12, f32[8192,128]{1,0:T(8,128)} %pack.1.table_hbm), custom_call_target="tpu_custom_call" | custom-call | tf_op jit(solution)/shard_map/gather/pallas_call | solution.py:605
  37.6 4.0 %all-to-all-start.1 = ((f32[128,1,640]{2,1,0:T(1,128)}), f32[128,1,640]{2,1,0:T(1,128)S(1)}, u32[]{:S(2)}, u32[]{:S(2)}) async-start(f32[128,1,640]{2,1,0:T(1,128)} %bitcast.4), calls=%async_computation.1 | async-start | bytes 655360 | tf_op jit(solution)/shard_map/all_to_all | solution.py:565
  41.6 0.0 copy-done.1
  41.6 0.0 copy-done.2
  41.6 0.6 marks.1
  42.3 10.9 %all-to-all-done.1 = f32[128,1,640]{2,1,0:T(1,128)S(1)} async-done(((f32[128,1,640]{2,1,0:T(1,128)}), f32[128,1,640]{2,1,0:T(1,128)S(1)}, u32[]{:S(2)}, u32[]{:S(2)}) %all-to-all-start.1) | async-done | bytes 327712 | tf_op jit(solution)/shard_map/all_to_all | solution.py:565
  53.2 0.0 copy-done
  53.2 13.3 %render.1 = (f32[4,4,256]{2,1,0:T(4,128)}, f32[640,128]{1,0:T(8,128)S(1)}) custom-call(f32[640,128]{1,0:T(8,128)S(1)} %bitcast.10, bf16[256,4096]{1,0:T(8,128)(2,1)S(1)} %get-tuple-element.18.hot_ref, bf16[32,4096]{1,0:T(8,128)(2,1)S(1)} %get-tuple-element.19.mark_ref, f32[32,128]{1,0:T(8,128)S(1)} %get-tuple-element.20.key_ref, f32[4,4,256]{2,1,0:T(4,128)S(1)} %copy-done), custom_call_target="tpu_custom_call" | custom-call | tf_op jit(solution)/shard_map/render/pallas_call | solution.py:626
  66.5 15.9 %all_to_all.15 = f32[128,1,640]{2,1,0:T(1,128)S(1)} all-to-all(f32[128,1,640]{2,1,0:T(1,128)S(1)} %bitcast.11), channel_id=1, replica_groups=mesh['row'=4,'col'=32] {'row','col'}, dimensions={0} | all-to-all | bytes 655360 | tf_op jit(solution)/shard_map/all_to_all | solution.py:565
  82.3 15.0 %scatter.1 = f32[10,65536]{1,0:T(8,128)} custom-call(s32[128,128]{1,0:T(8,128)S(1)} %get-tuple-element.17.after_ref.row_number_ref, bf16[512,128]{1,0:T(8,128)(2,1)S(1)} %get-tuple-element.22.group_ref, f32[640,128]{1,0:T(8,128)S(1)} %bitcast.9), custom_call_target="tpu_custom_call" | custom-call | tf_op jit(solution)/shard_map/scatter/pallas_call | solution.py:639
Async XLA Ops:
  4.1 21.1 %all-to-all-start = ((s32[128,1,128]{2,1,0:T(1,128)}), s32[128,1,128]{2,1,0:T(1,128)S(1)}, u32[]{:S(2)}, u32[]{:S(2)}) async-start(s32[128,1,128]{2,1,0:T(1,128)} %bitcast.13), calls=%async_computation | async-start | bytes 131072 | tf_op jit(solution)/shard_map/all_to_all | solution.py:565
  19.1 22.5 %copy-start.1 = (f32[32,128]{1,0:T(8,128)S(1)}, f32[32,128]{1,0:T(8,128)}, u32[]{:S(2)}) copy-start(f32[32,128]{1,0:T(8,128)} %get-tuple-element.15.owner_ref) | copy-start | bytes 49156
  19.2 22.5 %copy-start.2 = (f32[32,128]{1,0:T(8,128)S(1)}, f32[32,128]{1,0:T(8,128)}, u32[]{:S(2)}) copy-start(f32[32,128]{1,0:T(8,128)} %get-tuple-element.16.rank_ref) | copy-start | bytes 49156
  19.2 34.0 %copy-start = (f32[4,4,256]{2,1,0:T(4,128)S(1)}, f32[4,4,256]{2,1,0:T(4,128)}, u32[]{:S(2)}) copy-start(f32[4,4,256]{2,1,0:T(4,128)} %target_ref.1) | copy-start | bytes 49156
  37.6 15.6 %all-to-all-start.1 = ((f32[128,1,640]{2,1,0:T(1,128)}), f32[128,1,640]{2,1,0:T(1,128)S(1)}, u32[]{:S(2)}, u32[]{:S(2)}) async-start(f32[128,1,640]{2,1,0:T(1,128)} %bitcast.4), calls=%async_computation.1 | async-start | bytes 655360 | tf_op jit(solution)/shard_map/all_to_all | solution.py:565
